TPU v7x, 32 devices: a whole 2x2x4 slice. The times are simulated.
32 devices in a mesh: dp: 4 (over y, x), ctx: 8 (over z, core).
Axes of the slice: x: 2, y: 2, z: 4, core: 2. Of those that a mesh axis runs over, the one named last changes fastest.
Arguments:
- tokens: bfloat16 [8, 1024, 1024], P('dp', 'ctx'), may hold values from -6 to 6
- cotangent: bfloat16 [8, 1024, 1024], P('dp', 'ctx'), may hold values from -6 to 6
- segments: int32 [8, 1024], P('dp'), may hold values from 0 to 7, as said below
- span_order: int32 [8], replicated, may hold values from 0 to 7, each once
- w_query: bfloat16 [1024, 2048], P(('dp', 'ctx')), may hold values from -0.1875 to 0.1875
- key_weight: bfloat16 [1024, 1024], P(('dp', 'ctx')), may hold values from -0.1875 to 0.1875
- value_weight: bfloat16 [1024, 1024], P(('dp', 'ctx')), may hold values from -0.1875 to 0.1875
- w_output: bfloat16 [2048, 1024], P(('dp', 'ctx')), may hold values from -0.5 to 0.5
- w_gate: bfloat16 [1024, 3072], P(('dp', 'ctx')), may hold values from -0.1875 to 0.1875
- w_up: bfloat16 [1024, 3072], P(('dp', 'ctx')), may hold values from -0.1875 to 0.1875
- w_down: bfloat16 [3072, 1024], P(('dp', 'ctx')), may hold values from -0.109375 to 0.109375
- gains: bfloat16 [2304], P(('dp', 'ctx')), may hold values from 0.25 to 1.75
Outputs:
- result: bfloat16 [8, 1024, 1024], P('dp', 'ctx')
- input_grad: float32 [8, 1024, 1024], P('dp', 'ctx')
- grad_query: float32 [1024, 2048], P(('dp', 'ctx'))
- grad_key: float32 [1024, 1024], P(('dp', 'ctx'))
- grad_value: float32 [1024, 1024], P(('dp', 'ctx'))
- grad_output: float32 [2048, 1024], P(('dp', 'ctx'))
- grad_gate: float32 [1024, 3072], P(('dp', 'ctx'))
- grad_up: float32 [1024, 3072], P(('dp', 'ctx'))
- grad_down: float32 [3072, 1024], P(('dp', 'ctx'))
- grad_gains: float32 [2304], P(('dp', 'ctx'))
Inputs may be any that keep to these rules, and one draw needn't show every extreme that they name: `segments`: along each sequence the numbers start at 0 and rise by 0 or 1 from one position to the next; a run of equal numbers is one document. `span_order`: each slot number appears once.
All inputs are finite; a program needn't handle non-finite values.
Results may differ from a plain program's by a relative error of at most 0.015.
Values may be sent and summed in bfloat16 or wider, within the bound.
A program may use at most 256 MiB of HBM per device.

v0:
```python
import math

import jax
import jax.numpy as jnp
from jax import lax
from jax.sharding import PartitionSpec as P

QUERY_HEADS = 16
KEY_VALUE_HEADS = 8
HEAD_SIZE = 128


norm_eps = 1e-06
rope_base = 1000000.0
masked_score = -1e30


def rms_scale(value_rows, gain):
    return (
        value_rows
        * lax.rsqrt(jnp.mean(value_rows * value_rows, axis=-1, keepdims=True) + norm_eps)
        * gain
    )


def rotate(value_rows, positions):
    half = value_rows.shape[-1] // 2
    freq = rope_base ** (-(jnp.arange(half).astype(jnp.float32) * 2.0 / value_rows.shape[-1]))
    angle = positions.astype(jnp.float32)[:, None] * freq[None, :]
    cosine = jnp.cos(angle)[:, None, :]
    sine = jnp.sin(angle)[:, None, :]
    first_half = value_rows[..., :half]
    second_half = value_rows[..., half:]
    return jnp.concatenate(
        [first_half * cosine - second_half * sine, second_half * cosine + first_half * sine],
        axis=-1,
    )


def token_layout(segments, span_order, token_span):
    row_count, segment_length = segments.shape
    spots = jnp.arange(segment_length, dtype=jnp.int32)
    opens = jnp.concatenate(
        [jnp.ones((row_count, 1), dtype=jnp.bool_), segments[:, 1:] != segments[:, :-1]], axis=1
    )
    firsts = lax.cummax(jnp.where(opens, spots[None, :], jnp.int32(0)), axis=1)
    in_doc = spots[None, :] - firsts
    true_index = (
        span_order[:, None] * token_span + jnp.arange(token_span, dtype=jnp.int32)[None, :]
    ).reshape(segment_length)
    return (
        true_index,
        jnp.take(segments, true_index, axis=1),
        jnp.take(in_doc, true_index, axis=1),
    )


def swiglu(gate, up_part):
    return gate * jax.nn.sigmoid(gate) * up_part


def scores_of(q_seq, k_seq, allowed):
    score_scale = 1.0 / math.sqrt(q_seq.shape[-1])
    scores = (
        jnp.einsum("qhgd,khd->hgqk", q_seq, k_seq, preferred_element_type=jnp.float32) * score_scale
    )
    return jnp.where(allowed[None, None], scores, masked_score)


def attend(items):
    q_seq, k_seq, v_seq, allowed = items
    scores = scores_of(q_seq, k_seq, allowed)
    top = jnp.max(scores, axis=-1, keepdims=True)
    expo = jnp.exp(scores - top)
    total = jnp.sum(expo, axis=-1, keepdims=True)
    probs_low = (expo / total).astype(jnp.bfloat16)
    mixed_seq = jnp.einsum("hgqk,khd->qhgd", probs_low, v_seq, preferred_element_type=jnp.float32)
    return (mixed_seq, top, total)


def attend_back(items):
    q_seq, k_seq, v_seq, allowed, top, total, grad_seq = items
    score_scale = 1.0 / math.sqrt(q_seq.shape[-1])
    scores = scores_of(q_seq, k_seq, allowed)
    probs = jnp.exp(scores - top) / total
    probs_low = probs.astype(jnp.bfloat16)
    d_probs = jnp.einsum("qhgd,khd->hgqk", grad_seq, v_seq, preferred_element_type=jnp.float32)
    inner = jnp.sum(probs * d_probs, axis=-1, keepdims=True)
    d_scores = (probs * (d_probs - inner)).astype(jnp.bfloat16)
    d_query = (
        jnp.einsum("hgqk,khd->qhgd", d_scores, k_seq, preferred_element_type=jnp.float32)
        * score_scale
    )
    d_key = (
        jnp.einsum("hgqk,qhgd->khd", d_scores, q_seq, preferred_element_type=jnp.float32)
        * score_scale
    )
    d_value = jnp.einsum("hgqk,qhgd->khd", probs_low, grad_seq, preferred_element_type=jnp.float32)
    segment_length = k_seq.shape[0]
    return (d_query, d_key.reshape(segment_length, -1), d_value.reshape(segment_length, -1))


def local(
    tokens,
    cotangent,
    segments,
    span_order,
    w_query,
    key_weight,
    value_weight,
    w_output,
    w_gate,
    w_up,
    w_down,
    gains,
):
    sequence_count, token_span, width = tokens.shape
    token_rows = sequence_count * token_span
    query_group = QUERY_HEADS // KEY_VALUE_HEADS
    key_value_width = KEY_VALUE_HEADS * HEAD_SIZE
    slot = lax.axis_index("ctx")
    true_index, seg_store, pos_store = token_layout(segments, span_order, token_span)
    query_index = lax.dynamic_slice_in_dim(true_index, slot * token_span, token_span, 0)
    query_segs = lax.dynamic_slice_in_dim(seg_store, slot * token_span, token_span, 1)
    query_pos = lax.dynamic_slice_in_dim(pos_store, slot * token_span, token_span, 1).reshape(
        token_rows
    )
    allowed = (query_segs[:, :, None] == seg_store[:, None, :]) & (
        true_index[None, None, :] <= query_index[None, :, None]
    )
    full_query, full_key, full_value, full_output, full_gate, full_up, full_down, full_gains = (
        lax.all_gather(w_query, ("dp", "ctx"), axis=0, tiled=True),
        lax.all_gather(key_weight, ("dp", "ctx"), axis=0, tiled=True),
        lax.all_gather(value_weight, ("dp", "ctx"), axis=0, tiled=True),
        lax.all_gather(w_output, ("dp", "ctx"), axis=0, tiled=True),
        lax.all_gather(w_gate, ("dp", "ctx"), axis=0, tiled=True),
        lax.all_gather(w_up, ("dp", "ctx"), axis=0, tiled=True),
        lax.all_gather(w_down, ("dp", "ctx"), axis=0, tiled=True),
        lax.all_gather(gains, ("dp", "ctx"), axis=0, tiled=True),
    )
    gain_all = full_gains.astype(jnp.float32)
    gain_one = gain_all[:width]
    gain_two = gain_all[width : 2 * width]
    gain_query = gain_all[2 * width : 2 * width + HEAD_SIZE]
    gain_key = gain_all[2 * width + HEAD_SIZE :]

    def head_path(lin_part, gain):
        return rotate(rms_scale(lin_part, gain), query_pos)

    inputs = tokens.reshape(token_rows, width).astype(jnp.float32)
    first_normed = rms_scale(inputs, gain_one).astype(jnp.bfloat16)
    q_lin = jnp.dot(first_normed, full_query, preferred_element_type=jnp.float32).reshape(
        token_rows, QUERY_HEADS, HEAD_SIZE
    )
    key_linear = jnp.dot(first_normed, full_key, preferred_element_type=jnp.float32).reshape(
        token_rows, KEY_VALUE_HEADS, HEAD_SIZE
    )
    values_low = jnp.dot(first_normed, full_value, preferred_element_type=jnp.float32).astype(
        jnp.bfloat16
    )
    query_rows = head_path(q_lin, gain_query).astype(jnp.bfloat16)
    keys = head_path(key_linear, gain_key).astype(jnp.bfloat16)
    gathered_keys, gathered_values = (
        lax.all_gather(
            keys.reshape(sequence_count, token_span, key_value_width), "ctx", axis=1, tiled=True
        ),
        lax.all_gather(
            values_low.reshape(sequence_count, token_span, key_value_width),
            "ctx",
            axis=1,
            tiled=True,
        ),
    )
    segment_length = gathered_keys.shape[1]
    query_sequences = query_rows.reshape(
        sequence_count, token_span, KEY_VALUE_HEADS, query_group, HEAD_SIZE
    )
    key_sequences = gathered_keys.reshape(
        sequence_count, segment_length, KEY_VALUE_HEADS, HEAD_SIZE
    )
    value_sequences = gathered_values.reshape(
        sequence_count, segment_length, KEY_VALUE_HEADS, HEAD_SIZE
    )
    mixed, tops, totals = lax.map(
        attend, (query_sequences, key_sequences, value_sequences, allowed)
    )
    mixed_low = mixed.reshape(token_rows, QUERY_HEADS * HEAD_SIZE).astype(jnp.bfloat16)
    middle = inputs + jnp.dot(mixed_low, full_output, preferred_element_type=jnp.float32)
    normed_two = rms_scale(middle, gain_two).astype(jnp.bfloat16)
    gate = jnp.dot(normed_two, full_gate, preferred_element_type=jnp.float32)
    up_part = jnp.dot(normed_two, full_up, preferred_element_type=jnp.float32)
    hidden = swiglu(gate, up_part).astype(jnp.bfloat16)
    result = (middle + jnp.dot(hidden, full_down, preferred_element_type=jnp.float32)).astype(
        jnp.bfloat16
    )
    full_query, full_key, full_value, full_output, full_gate, full_up, full_down = (
        lax.all_gather(w_query, ("dp", "ctx"), axis=0, tiled=True),
        lax.all_gather(key_weight, ("dp", "ctx"), axis=0, tiled=True),
        lax.all_gather(value_weight, ("dp", "ctx"), axis=0, tiled=True),
        lax.all_gather(w_output, ("dp", "ctx"), axis=0, tiled=True),
        lax.all_gather(w_gate, ("dp", "ctx"), axis=0, tiled=True),
        lax.all_gather(w_up, ("dp", "ctx"), axis=0, tiled=True),
        lax.all_gather(w_down, ("dp", "ctx"), axis=0, tiled=True),
    )
    grad_out = cotangent.reshape(token_rows, width).astype(jnp.float32)
    grad_ff = grad_out.astype(jnp.bfloat16)
    grad_down = jnp.einsum("tf,td->fd", hidden, grad_ff, preferred_element_type=jnp.float32)
    d_hidden = jnp.einsum("td,fd->tf", grad_ff, full_down, preferred_element_type=jnp.float32)
    unused_value, swiglu_back = jax.vjp(swiglu, gate, up_part)
    d_gate, d_up = swiglu_back(d_hidden)
    d_gate = d_gate.astype(jnp.bfloat16)
    d_up = d_up.astype(jnp.bfloat16)
    grad_gate = jnp.einsum("td,tf->df", normed_two, d_gate, preferred_element_type=jnp.float32)
    grad_up = jnp.einsum("td,tf->df", normed_two, d_up, preferred_element_type=jnp.float32)
    d_normed_two = jnp.einsum(
        "tf,df->td", d_gate, full_gate, preferred_element_type=jnp.float32
    ) + jnp.einsum("tf,df->td", d_up, full_up, preferred_element_type=jnp.float32)
    unused_two, norm_two_back = jax.vjp(rms_scale, middle, gain_two)
    d_middle_norm, grad_two = norm_two_back(d_normed_two)
    d_middle = grad_out + d_middle_norm
    d_attn = d_middle.astype(jnp.bfloat16)
    grad_output = jnp.einsum("tc,td->cd", mixed_low, d_attn, preferred_element_type=jnp.float32)
    mixed_gradient = jnp.einsum(
        "td,cd->tc", d_attn, full_output, preferred_element_type=jnp.float32
    ).astype(jnp.bfloat16)
    sequence_gradients = mixed_gradient.reshape(
        sequence_count, token_span, KEY_VALUE_HEADS, query_group, HEAD_SIZE
    )
    d_queries, key_terms, value_terms = lax.map(
        attend_back,
        (
            query_sequences,
            key_sequences,
            value_sequences,
            allowed,
            tops,
            totals,
            sequence_gradients,
        ),
    )
    keys_gradient, d_values = (
        lax.psum_scatter(
            key_terms.astype(jnp.bfloat16), "ctx", scatter_dimension=1, tiled=True
        ).astype(jnp.float32),
        lax.psum_scatter(
            value_terms.astype(jnp.bfloat16), "ctx", scatter_dimension=1, tiled=True
        ).astype(jnp.float32),
    )
    unused_query, query_back = jax.vjp(head_path, q_lin, gain_query)
    d_q_lin, grad_qnorm = query_back(d_queries.reshape(token_rows, QUERY_HEADS, HEAD_SIZE))
    unused_key, key_return_gradient = jax.vjp(head_path, key_linear, gain_key)
    key_linear_gradient, key_norm_gradient = key_return_gradient(
        keys_gradient.reshape(token_rows, KEY_VALUE_HEADS, HEAD_SIZE)
    )
    d_q_low = d_q_lin.reshape(token_rows, QUERY_HEADS * HEAD_SIZE).astype(jnp.bfloat16)
    d_k_low = key_linear_gradient.reshape(token_rows, key_value_width).astype(jnp.bfloat16)
    d_v_low = d_values.reshape(token_rows, key_value_width).astype(jnp.bfloat16)
    grad_query = jnp.einsum("td,tc->dc", first_normed, d_q_low, preferred_element_type=jnp.float32)
    grad_key = jnp.einsum("td,tc->dc", first_normed, d_k_low, preferred_element_type=jnp.float32)
    grad_value = jnp.einsum("td,tc->dc", first_normed, d_v_low, preferred_element_type=jnp.float32)
    d_normed_one = jnp.einsum("tc,dc->td", d_q_low, full_query, preferred_element_type=jnp.float32)
    d_normed_one = d_normed_one + jnp.einsum(
        "tc,dc->td", d_k_low, full_key, preferred_element_type=jnp.float32
    )
    d_normed_one = d_normed_one + jnp.einsum(
        "tc,dc->td", d_v_low, full_value, preferred_element_type=jnp.float32
    )
    unused_one, norm_one_back = jax.vjp(rms_scale, inputs, gain_one)
    d_input_norm, grad_one = norm_one_back(d_normed_one)
    input_grad = (d_middle + d_input_norm).reshape(sequence_count, token_span, width)
    grad_gains = jnp.concatenate([grad_one, grad_two, grad_qnorm, key_norm_gradient])
    owned = (
        lax.psum_scatter(grad_query, ("dp", "ctx"), scatter_dimension=0, tiled=True),
        lax.psum_scatter(grad_key, ("dp", "ctx"), scatter_dimension=0, tiled=True),
        lax.psum_scatter(grad_value, ("dp", "ctx"), scatter_dimension=0, tiled=True),
        lax.psum_scatter(grad_output, ("dp", "ctx"), scatter_dimension=0, tiled=True),
        lax.psum_scatter(grad_gate, ("dp", "ctx"), scatter_dimension=0, tiled=True),
        lax.psum_scatter(grad_up, ("dp", "ctx"), scatter_dimension=0, tiled=True),
        lax.psum_scatter(grad_down, ("dp", "ctx"), scatter_dimension=0, tiled=True),
        lax.psum_scatter(grad_gains, ("dp", "ctx"), scatter_dimension=0, tiled=True),
    )
    return (
        result.reshape(sequence_count, token_span, width),
        input_grad,
        owned[0],
        owned[1],
        owned[2],
        owned[3],
        owned[4],
        owned[5],
        owned[6],
        owned[7],
    )


def solution(mesh):
    return jax.shard_map(
        local,
        mesh=mesh,
        in_specs=(
            P("dp", "ctx", None),
            P("dp", "ctx", None),
            P("dp", None),
            P(),
            P(("dp", "ctx"), None),
            P(("dp", "ctx"), None),
            P(("dp", "ctx"), None),
            P(("dp", "ctx"), None),
            P(("dp", "ctx"), None),
            P(("dp", "ctx"), None),
            P(("dp", "ctx"), None),
            P(("dp", "ctx")),
        ),
        out_specs=(
            P("dp", "ctx", None),
            P("dp", "ctx", None),
            P(("dp", "ctx"), None),
            P(("dp", "ctx"), None),
            P(("dp", "ctx"), None),
            P(("dp", "ctx"), None),
            P(("dp", "ctx"), None),
            P(("dp", "ctx"), None),
            P(("dp", "ctx"), None),
            P(("dp", "ctx")),
        ),
        check_vma=False,
    )
```

profile of v0, /device:TPU:0, one launch (start us, length us, event | category | flops | bytes accessed | tf_op | source)
XLA Modules:
  0.0 1917.5 jit_solution(5272209031667979334)
XLA Ops:
  12.5 2.8 gather_fusion.1
  16.3 42.1 %all-reduce.5 = bf16[2304]{0:T(1024)(128)(2,1)S(1)} all-reduce(bf16[2304]{0:T(1024)(128)(2,1)S(1)} %dynamic-update-slice), channel_id=1, replica_groups=mesh['dp'=4,'ctx'=8] {'dp','ctx'}, use_global_device_ids=true, to_apply=%add.5 | all-reduce | flops 2304 | bytes 9216
  61.5 8.7 all-gather.14.cloned.1.call-done
  70.2 2.9 copy.108
  76.7 52.0 %all-gather.10.cloned.1.call-done = bf16[1024,1024]{1,0:T(8,128)(2,1)} async-done(((bf16[32,1024]{1,0:T(8,128)(2,1)}), bf16[1024,1024]{1,0:T(8,128)(2,1)}) %all-gather.10.cloned.1.call-update) | async-done | bytes 2097168 | tf_op jit(solution)/shard_map/all_gather | solution.py:134
  139.6 53.2 %all-gather.18.cloned.1.call-done = bf16[1024,2048]{1,0:T(8,128)(2,1)} async-done(((bf16[32,2048]{1,0:T(8,128)(2,1)}), bf16[1024,2048]{1,0:T(8,128)(2,1)}) %all-gather.18.cloned.1.call-update) | async-done | bytes 4194320 | tf_op jit(solution)/shard_map/all_gather | solution.py:132
  192.7 6.4 copy.112
  199.2 3.9 multiply_reduce_fusion.2
  207.5 2.8 pad_maximum_fusion
  210.3 30.3 %all-gather.16.cloned.1.call-done = bf16[2,1024,1024]{1,2,0:T(8,128)(2,1)} async-done(((bf16[2,128,1024]{1,2,0:T(8,128)(2,1)}), bf16[2,1024,1024]{1,2,0:T(8,128)(2,1)}) %all-gather.16.cloned.1.call-update) | async-done | bytes 4194320 | tf_op jit(solution)/shard_map/all_gather | solution.py:164
  240.6 6.3 copy.115
  246.9 41.7 %all-gather.12.cloned.1.call-done = bf16[2,1024,1024]{1,2,0:T(8,128)(2,1)} async-done(((bf16[2,128,1024]{1,2,0:T(8,128)(2,1)}), bf16[2,1024,1024]{1,2,0:T(8,128)(2,1)}) %all-gather.12.cloned.1.call-update) | async-done | bytes 4194320 | tf_op jit(solution)/shard_map/all_gather | solution.py:167
  288.6 15.7 while.28
  288.7 3.0 fusion.142
  296.5 3.1 fusion.142
  308.6 43.2 %all-gather.20.cloned.1.call-done = bf16[2048,1024]{1,0:T(8,128)(2,1)} async-done(((bf16[64,1024]{1,0:T(8,128)(2,1)}), bf16[2048,1024]{1,0:T(8,128)(2,1)}) %all-gather.20.cloned.1.call-update) | async-done | bytes 4194320 | tf_op jit(solution)/shard_map/all_gather | solution.py:135
  351.9 3.5 multiply_reduce_fusion.7
  356.6 66.3 %all-gather.22.cloned.1.call-done = bf16[1024,3072]{1,0:T(8,128)(2,1)} async-done(((bf16[32,3072]{1,0:T(8,128)(2,1)}), bf16[1024,3072]{1,0:T(8,128)(2,1)}) %all-gather.22.cloned.1.call-update) | async-done | bytes 6291472 | tf_op jit(solution)/shard_map/all_gather | solution.py:136
  422.9 6.2 fusion.75
  429.1 64.8 %all-gather.24.cloned.1.call-done = bf16[1024,3072]{1,0:T(8,128)(2,1)} async-done(((bf16[32,3072]{1,0:T(8,128)(2,1)}), bf16[1024,3072]{1,0:T(8,128)(2,1)}) %all-gather.24.cloned.1.call-update) | async-done | bytes 6291472 | tf_op jit(solution)/shard_map/all_gather | solution.py:137
  493.9 6.2 fusion.76
  500.1 64.7 %all-gather.26.cloned.1.call-done = bf16[3072,1024]{1,0:T(8,128)(2,1)} async-done(((bf16[96,1024]{1,0:T(8,128)(2,1)}), bf16[3072,1024]{1,0:T(8,128)(2,1)}) %all-gather.26.cloned.1.call-update) | async-done | bytes 6291472 | tf_op jit(solution)/shard_map/all_gather | solution.py:138
  564.8 9.8 multiply_convert_fusion
  574.6 5.8 fusion.77
  580.7 2.9 multiply_reduce_fusion.4
  587.8 131.2 %while.29 = (s32[]{:T(128)}, f32[2,128,8,2,128]{1,0,4,3,2:T(2,128)}, bf16[2,1024,1024]{1,2,0:T(8,128)(2,1)}, bf16[2,1024,1024]{2,1,0:T(8,128)(2,1)}, bf16[2,1024...) while((s32[]{:T(128)}, ...), condition=%wide.region_13.15_spmd, body=%wide.region_11.14_spmd.sunk | while | flops 2707683328 | bytes 193398064 | solution.py:229
  589.4 3.0 fusion.151
  592.5 6.3 fusion.152
  598.9 6.9 fusion.153
  605.8 4.1 fusion.154
  609.9 26.6 %dynamic_update_slice.35 = f32[2,128,8,2,128]{1,0,4,3,2:T(2,128)} dynamic-update-slice(f32[2,128,8,2,128]{1,0,4,3,2:T(2,128)} %get-tuple-element.448, f32[1,128,8,2,128]{1,0,4,3,2:T(1,128)S(1)} %bitcast.296, s32[]{:T(128)S(6)} %copy.201, s32[]{:T(128)} %constant.64.clone.1..sunk, s32[]{:T(128)} %constant.64.clone.1..sunk, s32[]{:T(128)} %constant.64.clone.1..sunk, s32[]{:T(128)} %constant.64.clone.1..sunk) | dynamic-update-slice | bytes 2097156 | tf_op jit(solution)/shard_map/while/body/jit(dynamic_update_index_in_dim)/dynamic_update_slice | solution.py:184
  636.5 4.0 bitcast_multiply_fusion.6
  642.9 6.2 fusion.155
  649.1 2.9 copy.177
  654.9 3.0 fusion.151
  658.0 6.3 fusion.152
  664.3 6.9 fusion.153
  671.3 4.1 fusion.154
  675.4 26.6 %dynamic_update_slice.35 = f32[2,128,8,2,128]{1,0,4,3,2:T(2,128)} dynamic-update-slice(f32[2,128,8,2,128]{1,0,4,3,2:T(2,128)} %get-tuple-element.448, f32[1,128,8,2,128]{1,0,4,3,2:T(1,128)S(1)} %bitcast.296, s32[]{:T(128)S(6)} %copy.201, s32[]{:T(128)} %constant.64.clone.1..sunk, s32[]{:T(128)} %constant.64.clone.1..sunk, s32[]{:T(128)} %constant.64.clone.1..sunk, s32[]{:T(128)} %constant.64.clone.1..sunk) | dynamic-update-slice | bytes 2097156 | tf_op jit(solution)/shard_map/while/body/jit(dynamic_update_index_in_dim)/dynamic_update_slice | solution.py:184
  702.0 4.0 bitcast_multiply_fusion.6
  708.4 6.2 fusion.155
  714.6 2.9 copy.177
  719.0 11.3 copy.141
  730.3 5.7 copy.166
  736.9 4.3 reshape.366
  745.5 4.6 fusion.79
  751.6 4.6 fusion.64
  757.2 7.8 fusion.81
  765.2 7.8 fusion.82
  774.0 7.9 fusion.83
  790.0 3.2 reshape.372
  795.3 2.8 fusion.80
  798.2 36.9 %reduce-scatter.12.cloned.1.call-done = bf16[2,128,1024]{2,1,0:T(8,128)(2,1)} async-done(((bf16[2,1024,1024]{2,1,0:T(8,128)(2,1)}), bf16[2,128,1024]{2,1,0:T(8,128)(2,1)}) %reduce-scatter.12.cloned.1.call-update) | async-done | bytes 524304 | tf_op jit(solution)/shard_map/reduce_scatter | solution.py:245
  835.2 3.8 convolution_bitcast_fusion
  839.0 3.6 fusion.78
  842.7 5.6 fusion.52
  851.2 39.1 %all-reduce.6 = f32[2304]{0:T(1024)S(1)} all-reduce(f32[2304]{0:T(1024)S(1)} %pad_maximum_fusion.2), channel_id=11, replica_groups=mesh['dp'=4,'ctx'=8] {'dp','ctx'}, use_global_device_ids=true, to_apply=%region_30.32.clone | all-reduce | flops 2304 | bytes 18432
  892.2 96.3 %reduce-scatter.14.cloned.1.call-done = f32[32,2048]{1,0:T(8,128)} async-done(((f32[1024,2048]{1,0:T(8,128)}), f32[32,2048]{1,0:T(8,128)}) %reduce-scatter.14.cloned.1.call-update) | async-done | bytes 262160 | tf_op jit(solution)/shard_map/reduce_scatter | solution.py:273
  988.5 152.4 %reduce-scatter.20.cloned.1.call-done = f32[64,1024]{1,0:T(8,128)} async-done(((f32[2048,1024]{1,0:T(8,128)}), f32[64,1024]{1,0:T(8,128)}) %reduce-scatter.20.cloned.1.call-update) | async-done | bytes 262160 | tf_op jit(solution)/shard_map/reduce_scatter | solution.py:276
  1140.9 159.7 %reduce-scatter.22.cloned.1.call-done = f32[32,3072]{1,0:T(8,128)} async-done(((f32[1024,3072]{1,0:T(8,128)}), f32[32,3072]{1,0:T(8,128)}) %reduce-scatter.22.cloned.1.call-update) | async-done | bytes 393232 | tf_op jit(solution)/shard_map/reduce_scatter | solution.py:277
  1300.6 161.9 %reduce-scatter.24.cloned.1.call-done = f32[32,3072]{1,0:T(8,128)} async-done(((f32[1024,3072]{1,0:T(8,128)}), f32[32,3072]{1,0:T(8,128)}) %reduce-scatter.24.cloned.1.call-update) | async-done | bytes 393232 | tf_op jit(solution)/shard_map/reduce_scatter | solution.py:278
  1462.5 160.9 %reduce-scatter.26.cloned.1.call-done = f32[96,1024]{1,0:T(8,128)} async-done(((f32[3072,1024]{1,0:T(8,128)}), f32[96,1024]{1,0:T(8,128)}) %reduce-scatter.26.cloned.1.call-update) | async-done | bytes 393232 | tf_op jit(solution)/shard_map/reduce_scatter | solution.py:279
  1623.4 144.6 %reduce-scatter.16.cloned.1.call-done = f32[32,1024]{1,0:T(8,128)} async-done(((f32[1024,1024]{1,0:T(8,128)}), f32[32,1024]{1,0:T(8,128)}) %reduce-scatter.16.cloned.1.call-update) | async-done | bytes 131088 | tf_op jit(solution)/shard_map/reduce_scatter | solution.py:274
  1768.0 142.2 %reduce-scatter.18.cloned.1.call-done = f32[32,1024]{1,0:T(8,128)} async-done(((f32[1024,1024]{1,0:T(8,128)}), f32[32,1024]{1,0:T(8,128)}) %reduce-scatter.18.cloned.1.call-update) | async-done | bytes 131088 | tf_op jit(solution)/shard_map/reduce_scatter | solution.py:275
  (270 shorter events, 81.3 us)
Async XLA Ops:
  7.2 63.0 %all-gather.14.cloned.1.call-start = ((), (), s32[]{:S(2)}) async-start(), calls=%async_computation.11 | async-start | bytes 2162688 | tf_op jit(solution)/shard_map/all_gather | solution.py:133
  7.9 120.8 %all-gather.10.cloned.1.call-start = ((), (), s32[]{:S(2)}) async-start(), calls=%async_computation.9 | async-start | bytes 2162688 | tf_op jit(solution)/shard_map/all_gather | solution.py:134
  8.7 184.1 %all-gather.18.cloned.1.call-start = ((), (), s32[]{:S(2)}) async-start(), calls=%async_computation.13 | async-start | bytes 4325376 | tf_op jit(solution)/shard_map/all_gather | solution.py:132
  9.4 231.2 %all-gather.16.cloned.1.call-start = ((), (), s32[]{:S(2)}) async-start(), calls=%async_computation.12 | async-start | bytes 4718592 | tf_op jit(solution)/shard_map/all_gather | solution.py:164
  59.8 16.6 copy-start.49
  59.8 14.1 copy-start.53
  59.8 143.3 %copy-start.55 = (f32[128]{0:T(128)}, f32[128]{0:T(128)S(1)}, u32[]{:S(2)}) copy-start(f32[128]{0:T(128)S(1)} %get-tuple-element.263) | copy-start | bytes 1540
  59.9 16.6 copy-start.42
  60.2 144.6 %copy-start.31 = (f32[256,64]{0,1:T(8,128)}, f32[256,64]{0,1:T(8,128)S(1)}, u32[]{:S(2)}) copy-start(f32[256,64]{0,1:T(8,128)S(1)} %get-tuple-element.265) | copy-start | bytes 196612
  60.2 144.6 %copy-start.33 = (f32[256,64]{0,1:T(8,128)}, f32[256,64]{0,1:T(8,128)S(1)}, u32[]{:S(2)}) copy-start(f32[256,64]{0,1:T(8,128)S(1)} %get-tuple-element.266) | copy-start | bytes 196612
  61.5 137.7 %copy-start.4 = (bf16[2,128,1024]{2,1,0:T(8,128)(2,1)}, bf16[2,128,1024]{2,1,0:T(8,128)(2,1)S(1)}, u32[]{:S(2)}) copy-start(bf16[2,128,1024]{2,1,0:T(8,128)(2,1)S(1)} %fusion.62) | copy-start | bytes 1572868
  73.8 2.6 copy-start.10
  75.5 59.7 %copy-start.44 = (s32[2,1024]{1,0:T(2,128)S(1)}, s32[2,1024]{1,0:T(2,128)}, u32[]{:S(2)}) copy-start(s32[2,1024]{1,0:T(2,128)} %param.20) | copy-start | bytes 24580
  76.4 212.3 %all-gather.12.cloned.1.call-start = ((), (), s32[]{:S(2)}) async-start(), calls=%async_computation.10 | async-start | bytes 4718592 | tf_op jit(solution)/shard_map/all_gather | solution.py:167
  76.5 62.0 %copy-start.51 = (f32[256]{0:T(256)}, f32[256]{0:T(256)S(1)}, u32[]{:S(2)}) copy-start(f32[256]{0:T(256)S(1)} %bitcast_rsqrt_fusion) | copy-start | bytes 3076
  132.0 219.8 %all-gather.20.cloned.1.call-start = ((), (), s32[]{:S(2)}) async-start(), calls=%async_computation.14 | async-start | bytes 4325376 | tf_op jit(solution)/shard_map/all_gather | solution.py:135
  132.6 290.3 %all-gather.22.cloned.1.call-start = ((), (), s32[]{:S(2)}) async-start(), calls=%async_computation.15 | async-start | bytes 6488064 | tf_op jit(solution)/shard_map/all_gather | solution.py:136
  133.4 360.5 %all-gather.24.cloned.1.call-start = ((), (), s32[]{:S(2)}) async-start(), calls=%async_computation.16 | async-start | bytes 6488064 | tf_op jit(solution)/shard_map/all_gather | solution.py:137
  134.1 430.7 %all-gather.26.cloned.1.call-start = ((), (), s32[]{:S(2)}) async-start(), calls=%async_computation.17 | async-start | bytes 6488064 | tf_op jit(solution)/shard_map/all_gather | solution.py:138
  134.9 649.8 %reduce-scatter.28.cloned.1.call-start = ((), (), s32[]{:S(2)}) async-start(), calls=%async_computation.26 | async-start | bytes 4718592
  240.6 48.1 %copy-start.37 = (bf16[2,128,8,2,128]{1,4,3,2,0:T(8,128)(2,1)S(1)}, bf16[2,128,8,2,128]{1,4,3,2,0:T(8,128)(2,1)}, u32[]{:S(2)}) copy-start(bf16[2,128,8,2,128]{1,4,3,2,0:T(8,128)(2,1)} %custom-call.4) | copy-start | bytes 3145732
  291.7 2.2 copy-start.3
  299.6 2.2 copy-start.3
  308.6 47.9 %copy-start.15 = (bf16[256,2048]{1,0:T(8,128)(2,1)}, bf16[256,2048]{1,0:T(8,128)(2,1)S(1)}, u32[]{:S(2)}) copy-start(bf16[256,2048]{1,0:T(8,128)(2,1)S(1)} %convert_element_type.142) | copy-start | bytes 3145732
  356.6 137.3 %copy-start.17 = (bf16[256,1024]{1,0:T(8,128)(2,1)}, bf16[256,1024]{1,0:T(8,128)(2,1)S(1)}, u32[]{:S(2)}) copy-start(bf16[256,1024]{1,0:T(8,128)(2,1)S(1)} %multiply_convert_fusion.2) | copy-start | bytes 1572868
  429.1 135.7 %copy-start.27 = (bf16[2,128,1024]{2,1,0:T(8,128)(2,1)S(1)}, bf16[2,128,1024]{2,1,0:T(8,128)(2,1)}, u32[]{:S(2)}) copy-start(bf16[2,128,1024]{2,1,0:T(8,128)(2,1)} %param.19) | copy-start | bytes 1572868
  574.6 5.8 copy-start.36
  574.6 5.8 copy-start.35
  574.6 5.8 copy-start.24
  574.6 6.0 copy-start.58
  580.7 4.3 copy-start.59
  589.4 3.1 copy-start.2
  592.5 6.4 copy-start.1
  605.8 4.1 copy-start
  636.5 4.0 copy-start.19
  654.9 3.1 copy-start.2
  657.9 6.4 copy-start.1
  671.3 4.1 copy-start
  702.0 4.0 copy-start.19
  736.0 99.1 %reduce-scatter.12.cloned.1.call-start = ((), (), s32[]{:S(2)}) async-start(), calls=%async_computation.18 | async-start | bytes 4718592 | tf_op jit(solution)/shard_map/reduce_scatter | solution.py:245
  736.1 5.0 copy-start.32
  736.1 5.0 copy-start.34
  736.8 251.7 %reduce-scatter.14.cloned.1.call-start = ((), (), s32[]{:S(2)}) async-start(), calls=%async_computation.19 | async-start | bytes 8650752 | tf_op jit(solution)/shard_map/reduce_scatter | solution.py:273
  736.8 6.2 copy-start.7
  736.8 6.2 copy-start.39
  736.8 6.2 copy-start.56
  741.1 2.8 copy-start.48
  743.0 2.4 copy-start.5
  750.1 390.8 %reduce-scatter.20.cloned.1.call-start = ((), (), s32[]{:S(2)}) async-start(), calls=%async_computation.22 | async-start | bytes 8650752 | tf_op jit(solution)/shard_map/reduce_scatter | solution.py:276
  756.2 544.3 %reduce-scatter.22.cloned.1.call-start = ((), (), s32[]{:S(2)}) async-start(), calls=%async_computation.23 | async-start | bytes 12976128 | tf_op jit(solution)/shard_map/reduce_scatter | solution.py:277
  765.1 697.4 %reduce-scatter.24.cloned.1.call-start = ((), (), s32[]{:S(2)}) async-start(), calls=%async_computation.24 | async-start | bytes 12976128 | tf_op jit(solution)/shard_map/reduce_scatter | solution.py:278
  773.0 850.4 %reduce-scatter.26.cloned.1.call-start = ((), (), s32[]{:S(2)}) async-start(), calls=%async_computation.25 | async-start | bytes 12976128 | tf_op jit(solution)/shard_map/reduce_scatter | solution.py:279
  781.9 12.7 copy-start.9
  781.9 12.7 copy-start.41
  781.9 12.7 copy-start.54
  781.9 986.1 %reduce-scatter.16.cloned.1.call-start = ((), (), s32[]{:S(2)}) async-start(), calls=%async_computation.20 | async-start | bytes 4325376 | tf_op jit(solution)/shard_map/reduce_scatter | solution.py:274
  788.5 6.5 copy-start.46
  798.1 40.8 %copy-start.22 = (bf16[256,16,128]{0,2,1:T(8,128)(2,1)S(1)}, bf16[256,16,128]{0,2,1:T(8,128)(2,1)}, u32[]{:S(2)}) copy-start(bf16[256,16,128]{0,2,1:T(8,128)(2,1)} %copy-done.21) | copy-start | bytes 3145732
  798.2 1112.1 %reduce-scatter.18.cloned.1.call-start = ((), (), s32[]{:S(2)}) async-start(), calls=%async_computation.21 | async-start | bytes 4325376 | tf_op jit(solution)/shard_map/reduce_scatter | solution.py:275
  839.0 3.7 copy-start.25
  839.0 3.7 copy-start.30
  842.7 5.6 copy-start.14
  848.3 2.9 copy-start.57
  848.3 42.6 %copy-start.50 = (f32[2,128]{1,0:T(2,128)S(1)}, f32[2,128]{1,0:T(2,128)}, u32[]{:S(2)}) copy-start(f32[2,128]{1,0:T(2,128)} %copy-done.49) | copy-start | bytes 3076
  (20 other events, 29.0 us)
Sparse Core Ops, SparseCore 0:
  11.0 59.1 all-gather.13
  73.2 55.4 all-gather.9
  131.7 60.9 all-gather.17
  194.2 46.3 all-gather.15
  242.6 46.0 all-gather.11
  291.5 60.3 all-gather.19
  354.9 67.9 all-gather.21
  425.9 67.9 all-gather.23
  496.9 67.9 all-gather.25
  736.2 48.4 reduce-scatter.27
  787.0 48.1 reduce-scatter.11
  837.9 150.5 reduce-scatter.13
  991.4 149.4 reduce-scatter.19
  1147.3 153.1 reduce-scatter.21
  1308.0 154.4 reduce-scatter.23
  1469.0 154.4 reduce-scatter.25
  1626.2 141.7 reduce-scatter.15
  1770.8 139.3 reduce-scatter.17
where the time goes:
time: 1930 us; the launch traced here: 1920 us
  waiting for transfers between devices  1490 us (77%)
  matrix products  152 us (8%)
  local copies, waits for them, and re-layouts  144 us (7%)
  blocking collectives  81.2 us (4%)
  other arithmetic  35 us (2%)
    reduce_scatter x1, waiting for transfers between devices, local(): lax.psum_scatter(grad_up, ('dp', 'ctx'), scatter_dimension=0, tiled=True)  162 us
    reduce_scatter x1, waiting for transfers between devices, local(): lax.psum_scatter(grad_down, ('dp', 'ctx'), scatter_dimension=0, tiled=True)  161 us
    reduce_scatter x1, waiting for transfers between devices, local(): lax.psum_scatter(grad_gate, ('dp', 'ctx'), scatter_dimension=0, tiled=True)  160 us
    reduce_scatter x1, waiting for transfers between devices, local(): lax.psum_scatter(grad_output, ('dp', 'ctx'), scatter_dimension=0, tiled=T...  152 us
    reduce_scatter x1, waiting for transfers between devices, local(): lax.psum_scatter(grad_key, ('dp', 'ctx'), scatter_dimension=0, tiled=True)  145 us
    reduce_scatter x1, waiting for transfers between devices, local(): lax.psum_scatter(grad_value, ('dp', 'ctx'), scatter_dimension=0, tiled=True)  142 us
    reduce_scatter x1, waiting for transfers between devices, local(): lax.psum_scatter(grad_query, ('dp', 'ctx'), scatter_dimension=0, tiled=True)  96.3 us
    unnamed x2, blocking collectives  81.2 us
  transfers between devices with their start and end apart: 18, of which 18 were waited for; matrix products, arithmetic and copies ran while one was open for 8% of the time, Pallas kernels for 0%

commit v1 on v0

v1 whole, which is shorter than its diff:
```python
import math

import jax
import jax.numpy as jnp
from jax import lax
from jax.sharding import Mesh
from jax.sharding import PartitionSpec as P

QUERY_HEADS = 16
KEY_VALUE_HEADS = 8
HEAD_SIZE = 128


norm_eps = 1e-06
rope_base = 1000000.0
masked_score = -1e30


def rms_scale(value_rows, gain):
    return (
        value_rows
        * lax.rsqrt(jnp.mean(value_rows * value_rows, axis=-1, keepdims=True) + norm_eps)
        * gain
    )


def rotate(value_rows, positions):
    half = value_rows.shape[-1] // 2
    freq = rope_base ** (-(jnp.arange(half).astype(jnp.float32) * 2.0 / value_rows.shape[-1]))
    angle = positions.astype(jnp.float32)[:, None] * freq[None, :]
    cosine = jnp.cos(angle)[:, None, :]
    sine = jnp.sin(angle)[:, None, :]
    first_half = value_rows[..., :half]
    second_half = value_rows[..., half:]
    return jnp.concatenate(
        [first_half * cosine - second_half * sine, second_half * cosine + first_half * sine],
        axis=-1,
    )


def token_layout(segments, span_order, token_span):
    row_count, segment_length = segments.shape
    spots = jnp.arange(segment_length, dtype=jnp.int32)
    opens = jnp.concatenate(
        [jnp.ones((row_count, 1), dtype=jnp.bool_), segments[:, 1:] != segments[:, :-1]], axis=1
    )
    firsts = lax.cummax(jnp.where(opens, spots[None, :], jnp.int32(0)), axis=1)
    in_doc = spots[None, :] - firsts
    true_index = (
        span_order[:, None] * token_span + jnp.arange(token_span, dtype=jnp.int32)[None, :]
    ).reshape(segment_length)
    return (
        true_index,
        jnp.take(segments, true_index, axis=1),
        jnp.take(in_doc, true_index, axis=1),
    )


def swiglu(gate, up_part):
    return gate * jax.nn.sigmoid(gate) * up_part


SWAP = ((0, 1), (1, 0))


def swap(value):
    return lax.ppermute(value, "core", SWAP)


def local(
    tokens,
    cotangent,
    segments,
    span_order,
    w_query,
    key_weight,
    value_weight,
    w_output,
    w_gate,
    w_up,
    w_down,
    gains,
):
    sequence_count, token_span, width = tokens.shape
    token_rows = sequence_count * token_span
    group = QUERY_HEADS // KEY_VALUE_HEADS
    kv_width = KEY_VALUE_HEADS * HEAD_SIZE
    q_width = QUERY_HEADS * HEAD_SIZE
    core = lax.axis_index("core")
    first_core = core == 0
    chips = lax.axis_size("dp") * lax.axis_size("z")
    z_count = lax.axis_size("z")
    slot = lax.axis_index("z") * 2 + core
    f32, bf16 = jnp.float32, jnp.bfloat16

    def order(own, par, axis=-1):
        return jnp.concatenate(
            [jnp.where(first_core, own, par), jnp.where(first_core, par, own)], axis=axis
        )

    def halves(value):
        half = value.shape[-1] // 2
        a, b = value[..., :half], value[..., half:]
        return jnp.where(first_core, a, b), jnp.where(first_core, b, a)

    def chip_rows(parts):
        split = [halves(p) for p in parts]
        keep = jnp.concatenate([p[0] for p in split], axis=1)
        give = jnp.concatenate([p[1] for p in split], axis=1)
        return order(keep, swap(give), axis=0)

    def own_rows(value, sizes):
        rows = value.shape[0] // 2
        a, b = value[:rows], value[rows:]
        keep = jnp.where(first_core, a, b)
        got = swap(jnp.where(first_core, b, a))
        out, at = [], 0
        for size in sizes:
            out.append(order(keep[:, at : at + size], got[:, at : at + size]).astype(f32))
            at += size
        return out

    def gather(value):
        own = lax.all_gather(value, ("dp", "z"), axis=0, tiled=True)
        return own, swap(own)

    def scatter(own, par):
        total = (own + swap(par.astype(bf16)).astype(f32)).astype(bf16)
        return lax.psum_scatter(total, ("dp", "z"), scatter_dimension=0, tiled=True)

    def dot(a, b):
        return jnp.dot(a, b, preferred_element_type=f32)

    def dot_nt(a, b):
        return lax.dot_general(a, b, (((1,), (1,)), ((), ())), preferred_element_type=f32)

    def dot_tn(a, b):
        return lax.dot_general(a, b, (((0,), (0,)), ((), ())), preferred_element_type=f32)

    chip_qkv = chip_rows([w_query, key_weight, value_weight])
    chip_out = chip_rows([w_output])
    chip_gu = chip_rows([w_gate, w_up])
    chip_down = chip_rows([w_down])
    share = gains.shape[0]
    rows_chip = chip_qkv.shape[0]
    pad = jnp.pad(gains[None, :], ((0, rows_chip - 1), (0, 128 - share)))
    qkv_own, qkv_par = gather(jnp.concatenate([chip_qkv, pad], axis=1))
    lin_width = chip_qkv.shape[1]

    def gains_of(full):
        return full[::rows_chip, lin_width : lin_width + share]

    gain_all = order(gains_of(qkv_own)[:, None, :], gains_of(qkv_par)[:, None, :], axis=1)
    gain_all = gain_all.reshape(-1).astype(f32)
    gain_one = gain_all[:width]
    gain_two = gain_all[width : 2 * width]
    gain_query = gain_all[2 * width : 2 * width + HEAD_SIZE]
    gain_key = gain_all[2 * width + HEAD_SIZE :]

    true_index, seg_store, pos_store = token_layout(segments, span_order, token_span)
    query_index = lax.dynamic_slice_in_dim(true_index, slot * token_span, token_span, 0)
    query_segs = lax.dynamic_slice_in_dim(seg_store, slot * token_span, token_span, 1)
    query_pos = lax.dynamic_slice_in_dim(pos_store, slot * token_span, token_span, 1).reshape(
        token_rows
    )
    pairs_index = true_index.reshape(z_count, 2, token_span)
    key_index = order(pairs_index[:, 0], pairs_index[:, 1], axis=0).reshape(-1)
    pairs_segs = seg_store.reshape(sequence_count, z_count, 2, token_span)
    key_segs = order(pairs_segs[:, :, 0], pairs_segs[:, :, 1], axis=1).reshape(sequence_count, -1)
    allowed = (query_segs[:, :, None] == key_segs[:, None, :]) & (
        key_index[None, None, :] <= query_index[None, :, None]
    )

    def head_path(lin_part, gain):
        return rotate(rms_scale(lin_part, gain), query_pos)

    inputs = tokens.reshape(token_rows, width).astype(f32)
    first_normed = rms_scale(inputs, gain_one).astype(bf16)
    lin_own, lin_par = dot(first_normed, qkv_own), dot(first_normed, qkv_par)
    half_q, half_kv = q_width // 2, kv_width // 2

    def lin_slice(start, size):
        return order(lin_own[:, start : start + size], lin_par[:, start : start + size])

    q_lin = lin_slice(0, half_q).reshape(token_rows, QUERY_HEADS, HEAD_SIZE)
    key_linear = lin_slice(half_q, half_kv).reshape(token_rows, KEY_VALUE_HEADS, HEAD_SIZE)
    values_low = lin_slice(half_q + half_kv, half_kv).astype(bf16)
    query_rows = head_path(q_lin, gain_query).astype(bf16)
    keys = head_path(key_linear, gain_key).astype(bf16)

    kv = jnp.stack([keys.reshape(values_low.shape), values_low])
    kv = kv.reshape(2, sequence_count, token_span, KEY_VALUE_HEADS, HEAD_SIZE)
    kv = kv.transpose(0, 1, 3, 2, 4)
    kv_own = lax.all_gather(kv, "z", axis=0)
    kv_all = jnp.concatenate([kv_own, swap(kv_own)], axis=0)
    kv_all = kv_all.transpose(1, 2, 3, 0, 4, 5)
    key_count = kv_all.shape[3] * token_span
    kv_all = kv_all.reshape(2, sequence_count, KEY_VALUE_HEADS, key_count, HEAD_SIZE)
    k_all, v_all = kv_all[0], kv_all[1]

    out_own, out_par = gather(chip_out)
    gu_own, gu_par = gather(chip_gu)
    down_own, down_par = gather(chip_down)

    def to_heads(value):
        value = value.reshape(sequence_count, token_span, KEY_VALUE_HEADS, group, HEAD_SIZE)
        value = value.transpose(0, 2, 3, 1, 4)
        return value.reshape(sequence_count, KEY_VALUE_HEADS, group * token_span, HEAD_SIZE)

    def from_heads(value):
        value = value.reshape(sequence_count, KEY_VALUE_HEADS, group, token_span, HEAD_SIZE)
        return value.transpose(0, 3, 1, 2, 4).reshape(token_rows, q_width)

    score_scale = 1.0 / math.sqrt(HEAD_SIZE)
    q_heads = to_heads(query_rows)
    mask = jnp.concatenate([allowed] * group, axis=1)[:, None]
    scores = jnp.einsum("shqd,shkd->shqk", q_heads, k_all, preferred_element_type=f32)
    scores = jnp.where(mask, scores * score_scale, masked_score)
    top = jnp.max(scores, axis=-1, keepdims=True)
    expo = jnp.exp(scores - top)
    probs = expo / jnp.sum(expo, axis=-1, keepdims=True)
    probs_low = probs.astype(bf16)
    mixed = jnp.einsum("shqk,shkd->shqd", probs_low, v_all, preferred_element_type=f32)
    mixed_low = from_heads(mixed.astype(bf16))

    middle = inputs + order(dot(mixed_low, out_own), dot(mixed_low, out_par))
    normed_two = rms_scale(middle, gain_two).astype(bf16)
    both_own, both_par = dot(normed_two, gu_own), dot(normed_two, gu_par)
    ff_half = both_own.shape[1] // 2

    def hidden_of(both):
        return swiglu(both[:, :ff_half], both[:, ff_half:])

    hidden_own, hidden_back_own = jax.vjp(hidden_of, both_own)
    hidden_par, hidden_back_par = jax.vjp(hidden_of, both_par)
    hidden = order(hidden_own.astype(bf16), hidden_par.astype(bf16))
    result = (middle + order(dot(hidden, down_own), dot(hidden, down_par))).astype(bf16)

    grad_ff = cotangent.reshape(token_rows, width)
    grad_out = grad_ff.astype(f32)
    gff_own, gff_par = halves(grad_ff)
    s_down = scatter(dot_tn(hidden, gff_own), dot_tn(hidden, gff_par))
    d_hidden = dot_nt(gff_own, down_own) + dot_nt(gff_par, down_par)
    dh_own, dh_par = halves(d_hidden)
    d_both_own = hidden_back_own(dh_own)[0].astype(bf16)
    d_both_par = hidden_back_par(dh_par)[0].astype(bf16)
    s_gu = scatter(dot_tn(normed_two, d_both_own), dot_tn(normed_two, d_both_par))
    d_normed_two = dot_nt(d_both_own, gu_own) + dot_nt(d_both_par, gu_par)
    _, norm_two_back = jax.vjp(rms_scale, middle, gain_two)
    d_middle_norm, grad_two = norm_two_back(d_normed_two)
    d_middle = grad_out + d_middle_norm
    d_attn = d_middle.astype(bf16)
    da_own, da_par = halves(d_attn)
    s_out = scatter(dot_tn(mixed_low, da_own), dot_tn(mixed_low, da_par))
    d_mixed = (dot_nt(da_own, out_own) + dot_nt(da_par, out_par)).astype(bf16)
    g_heads = to_heads(d_mixed)

    d_probs = jnp.einsum("shqd,shkd->shqk", g_heads, v_all, preferred_element_type=f32)
    inner = jnp.sum(probs * d_probs, axis=-1, keepdims=True)
    d_scores = (probs * (d_probs - inner)).astype(bf16)
    d_queries = jnp.einsum("shqk,shkd->shqd", d_scores, k_all, preferred_element_type=f32)
    d_key = jnp.einsum("shqk,shqd->shkd", d_scores, q_heads, preferred_element_type=f32)
    d_value = jnp.einsum("shqk,shqd->shkd", probs_low, g_heads, preferred_element_type=f32)
    terms = jnp.stack([(d_key * score_scale).astype(bf16), d_value.astype(bf16)])
    terms = terms.reshape(
        2, sequence_count, KEY_VALUE_HEADS, 2 * z_count, token_span, HEAD_SIZE
    ).transpose(3, 0, 1, 2, 4, 5)
    terms_sum = (terms[:z_count].astype(f32) + swap(terms[z_count:]).astype(f32)).astype(bf16)
    d_kv = lax.psum_scatter(terms_sum, "z", scatter_dimension=0, tiled=False)
    d_kv = d_kv.transpose(0, 1, 3, 2, 4).astype(f32)
    d_queries = from_heads(d_queries * score_scale)

    _, query_back = jax.vjp(head_path, q_lin, gain_query)
    d_q_lin, grad_qnorm = query_back(d_queries.reshape(q_lin.shape))
    _, key_back = jax.vjp(head_path, key_linear, gain_key)
    d_k_lin, grad_knorm = key_back(d_kv[0].reshape(key_linear.shape))
    d_q_low = d_q_lin.reshape(token_rows, q_width).astype(bf16)
    d_k_low = d_k_lin.reshape(token_rows, kv_width).astype(bf16)
    d_v_low = d_kv[1].reshape(token_rows, kv_width).astype(bf16)
    split = [halves(d_q_low), halves(d_k_low), halves(d_v_low)]
    zeros = jnp.zeros((token_rows, 128), bf16)
    dl_own = jnp.concatenate([p[0] for p in split] + [zeros], axis=1)
    dl_par = jnp.concatenate([p[1] for p in split] + [zeros], axis=1)
    d_normed_one = dot_nt(dl_own, qkv_own) + dot_nt(dl_par, qkv_par)
    _, norm_one_back = jax.vjp(rms_scale, inputs, gain_one)
    d_input_norm, grad_one = norm_one_back(d_normed_one)
    input_grad = (d_middle + d_input_norm).reshape(sequence_count, token_span, width)

    grad_gains = jnp.concatenate([grad_one, grad_two, grad_qnorm, grad_knorm])
    grad_gains = grad_gains.reshape(chips, 2, share)

    def gain_block(part):
        block = jnp.pad(part[:, None, :], ((0, 0), (0, rows_chip - 1), (0, 128 - share)))
        return jnp.pad(block.reshape(width, 128), ((0, 0), (lin_width, 0)))

    gains_own = jnp.where(first_core, grad_gains[:, 0], grad_gains[:, 1])
    gains_par = jnp.where(first_core, grad_gains[:, 1], grad_gains[:, 0])
    s_qkv = scatter(
        dot_tn(first_normed, dl_own) + gain_block(gains_own),
        dot_tn(first_normed, dl_par) + gain_block(gains_par),
    )
    owned_gains = s_qkv[0, lin_width : lin_width + share].astype(f32)
    grad_query, grad_key, grad_value = own_rows(s_qkv[:, :lin_width], (half_q, half_kv, half_kv))
    (grad_output,) = own_rows(s_out, (width // 2,))
    grad_gate, grad_up = own_rows(s_gu, (ff_half, ff_half))
    (grad_down,) = own_rows(s_down, (width // 2,))
    return (
        result.reshape(sequence_count, token_span, width),
        input_grad,
        grad_query,
        grad_key,
        grad_value,
        grad_output,
        grad_gate,
        grad_up,
        grad_down,
        owned_gains,
    )


def solution(mesh):
    dp, ctx = mesh.devices.shape
    chips = Mesh(mesh.devices.reshape(dp, ctx // 2, 2), ("dp", "z", "core"))
    slots = ("z", "core")
    rows = P(("dp", "z", "core"), None)
    inner = jax.shard_map(
        local,
        mesh=chips,
        in_specs=(
            P("dp", slots, None),
            P("dp", slots, None),
            P("dp", None),
            P(),
            rows,
            rows,
            rows,
            rows,
            rows,
            rows,
            rows,
            P(("dp", "z", "core")),
        ),
        out_specs=(P("dp", slots, None), P("dp", slots, None))
        + (rows,) * 7
        + (P(("dp", "z", "core")),),
        check_vma=False,
    )
    return inner
```

time: 1930 us -> 1120 us (0.58)
  waiting for transfers between devices: 1490 us -> 821 us
  local copies, waits for them, and re-layouts: 144 us -> 61 us
  blocking collectives: 81.2 us -> 0 us
  other arithmetic: 35 us -> 78.6 us
  matrix products: 152 us -> 132 us
    reduce_scatter x8 -> x5, waiting for transfers between devices: 1050 us -> 441 us  [the longest x4 427 us: scatter(): return lax.psum_scatter(total, ('dp', 'z'), scatter_dimension=0, tiled=True)]
    unnamed x2 -> x0, blocking collectives: 81.2 us -> none
    all_gather x9 -> x5, waiting for transfers between devices: 425 us -> 349 us  [the longest x4 271 us: gather(): own = lax.all_gather(value, ('dp', 'z'), axis=0, tiled=True)]
    dynamic_update_slice x10 -> x0, local copies, waits for them, and re-layouts: 62.6 us -> none  [the longest x4 53.3 us: local(): lax.map(attend, (query_sequences, key_sequences, value_sequences, allowed))]
    ppermute x0 -> x18, waiting for transfers between devices: none -> 31.1 us  [swap(): return lax.ppermute(value, 'core', SWAP)]
    dot_general x35 -> x29, matrix products: 152 us -> 121 us  [the longest x8 27.4 us: dot_nt(): lax.dot_general(a, b, (((1,), (1,)), ((), ())), preferred_element_type=f32)]
    unnamed x117 -> x195, local copies, waits for them, and re-layouts: 32.6 us -> 12.5 us
  transfers between devices with their start and end apart: 18 -> 28, of which waited for: 18 -> 21; matrix products, arithmetic and copies ran while one was open for 8% -> 15% of each run, Pallas kernels for 0% -> 0%
where the time goes in v1:
time: 1120 us; the launch traced here: 1110 us
  waiting for transfers between devices  821 us (73%)
  matrix products  132 us (12%)
  other arithmetic  78.6 us (7%)
  local copies, waits for them, and re-layouts  61 us (5%)
  between operations  16.2 us (1%)
    reduce_scatter x4, waiting for transfers between devices, scatter(): return lax.psum_scatter(total, ('dp', 'z'), scatter_dimension=0, tiled=True)  427 us
    all_gather x4, waiting for transfers between devices, gather(): own = lax.all_gather(value, ('dp', 'z'), axis=0, tiled=True)  271 us
    all_gather x1, waiting for transfers between devices, local(): kv_own = lax.all_gather(kv, 'z', axis=0)  77.7 us
    ppermute x18, waiting for transfers between devices, swap(): return lax.ppermute(value, 'core', SWAP)  31.1 us
    dot_general x8, matrix products, dot_nt(): lax.dot_general(a, b, (((1,), (1,)), ((), ())), preferred_element_type=f32)  27.4 us
    dot_general x8, matrix products, dot_tn(): lax.dot_general(a, b, (((0,), (0,)), ((), ())), preferred_element_type=f32)  26.6 us
    dot_general x8, matrix products, dot(): return jnp.dot(a, b, preferred_element_type=f32)  24.2 us
  transfers between devices with their start and end apart: 28, of which 21 were waited for; matrix products, arithmetic and copies ran while one was open for 15% of the time, Pallas kernels for 0%

profile of v1, /device:TPU:0, one launch (start us, length us, event | category | flops | bytes accessed | tf_op | source)
XLA Modules:
  0.0 1113.9 jit_solution(3131465382815346909)
XLA Ops:
  12.9 80.8 %all-gather.7.cloned.1.call-done = bf16[1024,2176]{1,0:T(8,128)(2,1)} async-done(((bf16[64,2176]{1,0:T(8,128)(2,1)}), bf16[1024,2176]{1,0:T(8,128)(2,1)}) %all-gather.7.cloned.1.call-update) | async-done | bytes 4456464 | tf_op jit(solution)/shard_map/all_gather | solution.py:124
  95.4 5.2 collective-permute-done.7
  101.9 2.8 gather_fusion.1
  109.3 3.9 fusion.74
  124.9 43.3 %all-gather.13.cloned.1.call-done = bf16[3072,512]{1,0:T(8,128)(2,1)} async-done(((bf16[192,512]{1,0:T(8,128)(2,1)}), bf16[3072,512]{1,0:T(8,128)(2,1)}) %all-gather.13.cloned.1.call-update) | async-done | bytes 3145744 | tf_op jit(solution)/shard_map/all_gather | solution.py:124
  168.4 2.8 gather_fusion
  172.0 77.7 %all-gather.15.cloned.1.call-done = bf16[8,2,8,128,128]{4,3,2,1,0:T(8,128)(2,1)} async-done(((bf16[2,2,8,128,128]{4,3,2,1,0:T(8,128)(2,1)}), bf16[8,2,8,128,128]{4,3,2,1,0:T(8,128)(2,1)}) %all-gather.15.cloned.1.call-update) | async-done | bytes 4194320 | tf_op jit(solution)/shard_map/all_gather | solution.py:194
  249.7 4.8 copy.161
  255.6 56.6 %all-gather.9.cloned.1.call-done = bf16[2048,512]{1,0:T(8,128)(2,1)} async-done(((bf16[128,512]{1,0:T(8,128)(2,1)}), bf16[2048,512]{1,0:T(8,128)(2,1)}) %all-gather.9.cloned.1.call-update) | async-done | bytes 2097168 | tf_op jit(solution)/shard_map/all_gather | solution.py:124
  312.2 3.0 fusion.45
  315.3 2.7 convolution_add_fusion
  318.0 90.4 %all-gather.11.cloned.1.call-done = bf16[1024,3072]{1,0:T(8,128)(2,1)} async-done(((bf16[64,3072]{1,0:T(8,128)(2,1)}), bf16[1024,3072]{1,0:T(8,128)(2,1)}) %all-gather.11.cloned.1.call-update) | async-done | bytes 6291472 | tf_op jit(solution)/shard_map/all_gather | solution.py:124
  408.4 1.7 slice_select_fusion.3
  416.4 1.6 copy-done.11
  418.0 3.3 maximum_bitcast_fusion
  421.3 3.9 fusion.67
  425.2 11.5 %fusion.72 = (f32[2,8,256]{2,1,0:T(8,128)S(1)}, f32[2,8,256,1024]{3,2,1,0:T(8,128)}) fusion(pred[2,256,1024]{2,1,0:T(8,128)(4,1)S(1)} %pad_add_fusion.1, bf16[2,8,256,128]{3,2,1,0:T(8,128)(2,1)S(1)} %bitcast.228, bf16[2,8,1024,128]{3,2,1,0:T(8,128)(2,1)} %bitcast.224), kind=kOutput, calls=%fused_computation.275 | convolution fusion | flops 1090520064 | bytes 22560768 | tf_op jit(solution)/shard_map/sub | solution.py:220
  436.7 9.4 fusion.20
  448.1 2.7 fusion.75
  452.0 4.8 fusion.76
  456.8 5.7 fusion.77
  462.6 1.7 fusion.36
  464.4 6.9 fusion.43
  471.3 2.8 multiply_reduce_fusion.5
  475.5 2.5 fusion.47
  478.1 1.8 fusion.12
  479.8 1.8 reshape.374
  481.9 7.5 fusion.9
  489.4 11.7 %multiply_reduce_fusion = (f32[2,8,256]{2,1,0:T(8,128)S(1)}, f32[2,8,256,1024]{3,2,1,0:T(8,128)}) fusion(f32[2,8,256,1024]{3,2,1,0:T(8,128)} %get-tuple-element.112, f32[2,8,256]{2,1,0:T(8,128)S(1)} %get-tuple-element.111, bf16[2,8,256,128]{3,2,1,0:T(8,128)(2,1)S(1)} %bitcast.244, bf16[2,8,1024,128]{3,2,1,0:T(8,128)(2,1)} %bitcast.227), kind=kOutput, calls=%fused_computation.4 | convolution fusion | flops 1086320640 | bytes 38830080 | tf_op jit(solution)/shard_map/shqd,shkd->shqk/dot_general | solution.py:258
  501.1 5.5 copy.170
  506.7 11.9 %multiply_convert_fusion = bf16[2,8,256,1024]{3,2,1,0:T(8,128)(2,1)S(1)} fusion(f32[2,8,256,1024]{3,2,1,0:T(8,128)} %get-tuple-element.115, f32[2,8,256]{2,1,0:T(8,128)S(1)} %get-tuple-element.114, f32[2,8,256,1024]{3,2,1,0:T(8,128)} %get-tuple-element.112, f32[2,8,256]{2,1,0:T(8,128)S(1)} %get-tuple-element.111), kind=kLoop, calls=%fused_computation.3 | loop fusion | flops 16777216 | bytes 41975808 | tf_op jit(solution)/shard_map/convert_element_type | solution.py:260
  518.6 6.9 multiply_convert_fusion.1
  525.5 7.9 copy.169
  533.5 6.3 maximum_bitcast_fusion.1
  539.7 2.6 slice.371
  542.9 6.8 collective-permute-done.9
  549.7 3.1 add_convert_fusion.3
  556.1 4.7 broadcast_select_fusion.1
  560.8 2.1 add_convert_fusion.5
  564.4 2.6 convolution_convert_fusion.1
  567.6 4.4 convolution_convert_fusion
  572.8 2.7 add_convert_fusion.4
  575.6 6.9 collective-permute-done.14
  582.5 7.7 add_convert_fusion
  590.9 7.0 convolution_multiply_fusion
  598.0 1.6 copy.164
  601.2 2.9 multiply_reduce_fusion.1
  604.1 1.6 copy.165
  607.0 1.5 copy.166
  608.5 4.2 fusion.13
  614.0 14.0 %reduce-scatter.6.cloned.1.call-done = bf16[1,2,2,8,128,128]{5,3,4,2,1,0:T(8,128)(2,1)} async-done(((bf16[4,2,2,8,128,128]{5,3,4,2,1,0:T(8,128)(2,1)}), bf16[1,2,2,8,128,128]{5,3,4,2,1,0:T(8,128)(2,1)}) %reduce-scatter.6.cloned.1.call-update) | async-done | bytes 1048592 | tf_op jit(solution)/shard_map/reduce_scatter | solution.py:269
  632.7 2.3 fusion.26
  636.1 3.8 fusion.38
  640.0 3.9 fusion.32
  644.2 2.7 add_convert_fusion.2
  647.0 7.5 collective-permute-done.10
  654.5 3.6 add_convert_fusion.1
  659.2 3.2 fusion.63
  662.7 1.8 broadcast_select_fusion.14
  664.5 50.9 %reduce-scatter.10.cloned.1.call-done = bf16[128,512]{1,0:T(8,128)(2,1)} async-done(((bf16[2048,512]{1,0:T(8,128)(2,1)}), bf16[128,512]{1,0:T(8,128)(2,1)}) %reduce-scatter.10.cloned.1.call-update) | async-done | bytes 131088 | tf_op jit(solution)/shard_map/reduce_scatter | solution.py:129
  716.4 2.1 fusion.28
  718.5 129.7 %reduce-scatter.14.cloned.1.call-done = bf16[192,512]{1,0:T(8,128)(2,1)} async-done(((bf16[3072,512]{1,0:T(8,128)(2,1)}), bf16[192,512]{1,0:T(8,128)(2,1)}) %reduce-scatter.14.cloned.1.call-update) | async-done | bytes 196624 | tf_op jit(solution)/shard_map/reduce_scatter | solution.py:129
  852.3 146.9 %reduce-scatter.12.cloned.1.call-done = bf16[64,3072]{1,0:T(8,128)(2,1)} async-done(((bf16[1024,3072]{1,0:T(8,128)(2,1)}), bf16[64,3072]{1,0:T(8,128)(2,1)}) %reduce-scatter.12.cloned.1.call-update) | async-done | bytes 393232 | tf_op jit(solution)/shard_map/reduce_scatter | solution.py:129
  1002.8 99.5 %reduce-scatter.8.cloned.1.call-done = bf16[64,2176]{1,0:T(8,128)(2,1)} async-done(((bf16[1024,2176]{1,0:T(8,128)(2,1)}), bf16[64,2176]{1,0:T(8,128)(2,1)}) %reduce-scatter.8.cloned.1.call-update) | async-done | bytes 278544 | tf_op jit(solution)/shard_map/reduce_scatter | solution.py:129
  (380 shorter events, 69.2 us)
Async XLA Ops:
  7.2 86.5 %copy-start.57 = (bf16[96,1024]{1,0:T(8,128)(2,1)S(1)}, bf16[96,1024]{1,0:T(8,128)(2,1)}, u32[]{:S(2)}) copy-start(bf16[96,1024]{1,0:T(8,128)(2,1)} %param.24) | copy-start | bytes 589828
  7.2 87.1 %copy-start.72 = (s32[2,1024]{1,0:T(2,128)S(1)}, s32[2,1024]{1,0:T(2,128)}, u32[]{:S(2)}) copy-start(s32[2,1024]{1,0:T(2,128)} %param.16) | copy-start | bytes 24580
  7.2 94.5 %copy-start.89 = (s32[8]{0:T(128)S(1)}, s32[8]{0:T(128)}, u32[]{:S(2)}) copy-start(s32[8]{0:T(128)} %param.17) | copy-start | bytes 100
  7.2 86.4 %all-gather.7.cloned.1.call-start = ((), (), s32[]{:S(2)}) async-start(), calls=%async_computation.5 | async-start | bytes 4734976 | tf_op jit(solution)/shard_map/all_gather | solution.py:124
  9.8 1.5 collective-permute-start
  11.3 93.7 %copy-start.6 = (bf16[2,128,1024]{2,1,0:T(8,128)(2,1)S(1)}, bf16[2,128,1024]{2,1,0:T(8,128)(2,1)}, u32[]{:S(2)}) copy-start(bf16[2,128,1024]{2,1,0:T(8,128)(2,1)} %param.14) | copy-start | bytes 1572868
  12.8 155.4 %all-gather.13.cloned.1.call-start = ((), (), s32[]{:S(2)}) async-start(), calls=%async_computation.8 | async-start | bytes 3342336 | tf_op jit(solution)/shard_map/all_gather | solution.py:124
  93.6 13.7 %collective-permute-start.1 = (bf16[1024,2176]{1,0:T(8,128)(2,1)}, bf16[1024,2176]{1,0:T(8,128)(2,1)}, u32[]{:S(2)}, u32[]{:S(2)}) collective-permute-start(bf16[1024,2176]{1,0:T(8,128)(2,1)} %all-gather.7.cloned.1.call-done), channel_id=1, source_target_pairs={{0,1},{1,0},{2,3},{3,2},{4,5},{5,4},{6,7},{7,6},{8,9},{9,8},{10,11... | collective-permute-start | bytes 13369352 | tf_op jit(solution)/shard_map/ppermute | solution.py:67
  93.7 7.0 collective-permute-start.7
  101.4 148.3 %all-gather.15.cloned.1.call-start = ((), (), s32[]{:S(2)}) async-start(), calls=%async_computation.14 | async-start | bytes 5242880 | tf_op jit(solution)/shard_map/all_gather | solution.py:194
  105.7 7.5 copy-start.80
  106.3 308.1 %copy-start.34 = (f32[256,64]{1,0:T(8,128)}, f32[256,64]{1,0:T(8,128)S(1)}, u32[]{:S(2)}) copy-start(f32[256,64]{1,0:T(8,128)S(1)} %get-tuple-element.109) | copy-start | bytes 196612
  106.3 308.1 %copy-start.36 = (f32[256,64]{1,0:T(8,128)}, f32[256,64]{1,0:T(8,128)S(1)}, u32[]{:S(2)}) copy-start(f32[256,64]{1,0:T(8,128)S(1)} %get-tuple-element.110) | copy-start | bytes 196612
  109.1 4.1 copy-start.76
  120.0 192.2 %all-gather.9.cloned.1.call-start = ((), (), s32[]{:S(2)}) async-start(), calls=%async_computation.6 | async-start | bytes 2228224 | tf_op jit(solution)/shard_map/all_gather | solution.py:124
  120.1 1.3 collective-permute-start.3
  122.1 286.3 %all-gather.11.cloned.1.call-start = ((), (), s32[]{:S(2)}) async-start(), calls=%async_computation.7 | async-start | bytes 6684672 | tf_op jit(solution)/shard_map/all_gather | solution.py:124
  122.3 1.5 collective-permute-start.5
  124.7 503.4 %reduce-scatter.6.cloned.1.call-start = ((), (), s32[]{:S(2)}) async-start(), calls=%async_computation.9 | async-start | bytes 5242880 | tf_op jit(solution)/shard_map/reduce_scatter | solution.py:269
  168.2 144.0 %collective-permute-start.8 = (bf16[3072,512]{1,0:T(8,128)(2,1)}, bf16[3072,512]{1,0:T(8,128)(2,1)}, u32[]{:S(2)}, u32[]{:S(2)}) collective-permute-start(bf16[3072,512]{1,0:T(8,128)(2,1)} %all-gather.13.cloned.1.call-done), channel_id=1, source_target_pairs={{0,1},{1,0},{2,3},{3,2},{4,5},{5,4},{6,7},{7,6},{8,9},{9,8},{10,11... | collective-permute-start | bytes 9437192 | tf_op jit(solution)/shard_map/ppermute | solution.py:67
  249.7 62.5 %copy-start.47 = (bf16[2,128,1024]{2,1,0:T(8,128)(2,1)S(1)}, bf16[2,128,1024]{2,1,0:T(8,128)(2,1)}, u32[]{:S(2)}) copy-start(bf16[2,128,1024]{2,1,0:T(8,128)(2,1)} %param.15) | copy-start | bytes 1572868
  254.5 161.9 %collective-permute-start.2 = (bf16[4,2,2,8,128,128]{5,4,0,3,2,1:T(8,128)(2,1)}, bf16[4,2,2,8,128,128]{5,4,0,3,2,1:T(8,128)(2,1)}, u32[]{:S(2)}, u32[]{:S(2)}) collective-permute-start(bf16[4,2,2,8,128,128]{5,4,0,3,2,1:T(8,128)(2,1)} %copy.161), channel_id=1, source_target_pairs={{0,1},{1,0},{2,3},{3,2},{4,5},{5,4},{6,7},{7,6},{8,9},{9,8},{10,11... | collective-permute-start | bytes 12582920 | tf_op jit(solution)/shard_map/ppermute | solution.py:67
  312.2 135.9 %collective-permute-start.4 = (bf16[2048,512]{1,0:T(8,128)(2,1)}, bf16[2048,512]{1,0:T(8,128)(2,1)}, u32[]{:S(2)}, u32[]{:S(2)}) collective-permute-start(bf16[2048,512]{1,0:T(8,128)(2,1)} %all-gather.9.cloned.1.call-done), channel_id=1, source_target_pairs={{0,1},{1,0},{2,3},{3,2},{4,5},{5,4},{6,7},{7,6},{8,9},{9,8},{10,11... | collective-permute-start | bytes 6291464 | tf_op jit(solution)/shard_map/ppermute | solution.py:67
  408.4 48.4 %collective-permute-start.6 = (bf16[1024,3072]{1,0:T(8,128)(2,1)}, bf16[1024,3072]{1,0:T(8,128)(2,1)}, u32[]{:S(2)}, u32[]{:S(2)}) collective-permute-start(bf16[1024,3072]{1,0:T(8,128)(2,1)} %all-gather.11.cloned.1.call-done), channel_id=1, source_target_pairs={{0,1},{1,0},{2,3},{3,2},{4,5},{5,4},{6,7},{7,6},{8,9},{9,8},{10,11... | collective-permute-start | bytes 18874376 | tf_op jit(solution)/shard_map/ppermute | solution.py:67
  416.4 8.9 copy-start.33
  451.5 22.6 %copy-start.13 = (f32[256,512]{1,0:T(8,128)}, f32[256,512]{1,0:T(8,128)S(1)}, u32[]{:S(2)}) copy-start(f32[256,512]{1,0:T(8,128)S(1)} %get-tuple-element.53) | copy-start | bytes 1572868
  452.0 4.8 copy-start.20
  456.8 5.8 copy-start.16
  456.8 5.8 copy-start.15
  456.8 14.5 %slice-start = ((s8[6291456]{0:T(1024)(128)(4,1)}), s8[4194304]{0:T(1024)(128)(4,1)S(1)}, s32[]{:S(2)}) async-start(s8[6291456]{0:T(1024)(128)(4,1)} %bitcast.258), calls=%async_computation.15 | async-start | bytes 8388608
  462.6 8.7 slice-start.1
  464.3 6.9 copy-start.26
  464.3 6.9 copy-start.28
  464.3 6.9 copy-start.23
  464.4 6.9 copy-start.25
  518.6 6.9 copy-start.5
  525.5 7.9 copy-start.12
  539.7 10.0 copy-start.4
  542.4 7.4 collective-permute-start.9
  552.9 162.5 %reduce-scatter.10.cloned.1.call-start = ((), (), s32[]{:S(2)}) async-start(), calls=%async_computation.11 | async-start | bytes 2228224 | tf_op jit(solution)/shard_map/reduce_scatter | solution.py:129
  554.9 5.9 collective-permute-start.12
  563.0 285.3 %reduce-scatter.14.cloned.1.call-start = ((), (), s32[]{:S(2)}) async-start(), calls=%async_computation.13 | async-start | bytes 3342336 | tf_op jit(solution)/shard_map/reduce_scatter | solution.py:129
  564.4 8.4 copy-start.55
  567.0 5.8 copy-start.49
  567.0 5.8 copy-start.52
  567.1 5.8 collective-permute-start.16
  572.0 10.5 collective-permute-start.14
  575.5 7.0 copy-start.24
  575.5 423.7 %reduce-scatter.12.cloned.1.call-start = ((), (), s32[]{:S(2)}) async-start(), calls=%async_computation.12 | async-start | bytes 6684672 | tf_op jit(solution)/shard_map/reduce_scatter | solution.py:129
  590.2 512.1 %reduce-scatter.8.cloned.1.call-start = ((), (), s32[]{:S(2)}) async-start(), calls=%async_computation.10 | async-start | bytes 4734976 | tf_op jit(solution)/shard_map/reduce_scatter | solution.py:129
  601.2 4.4 copy-start.71
  635.3 4.7 copy-start.64
  635.3 4.7 copy-start.66
  635.3 4.7 copy-start.67
  644.1 10.3 copy-start.61
  644.2 10.3 copy-start.65
  646.9 7.6 collective-permute-start.10
  662.7 53.7 %copy-start.14 = (f32[256,512]{1,0:T(8,128)S(1)}, f32[256,512]{1,0:T(8,128)}, u32[]{:S(2)}) copy-start(f32[256,512]{1,0:T(8,128)} %copy-done.13) | copy-start | bytes 1572868
  716.3 2.2 collective-permute-start.13
  716.4 135.9 %copy-start.79 = (f32[2,128]{1,0:T(2,128)S(1)}, f32[2,128]{1,0:T(2,128)}, u32[]{:S(2)}) copy-start(f32[2,128]{1,0:T(2,128)} %copy-done.78) | copy-start | bytes 3076
  718.5 281.9 %copy-start.32 = (f32[256,1024]{1,0:T(8,128)S(1)}, f32[256,1024]{1,0:T(8,128)}, u32[]{:S(2)}) copy-start(f32[256,1024]{1,0:T(8,128)} %get-tuple-element.20) | copy-start | bytes 3145732
  849.2 1.4 collective-permute-start.17
  1000.3 1.5 collective-permute-start.15
  1103.3 1.4 collective-permute-start.11
  (56 other events, 130.7 us)
Sparse Core Ops, SparseCore 0:
  12.9 80.6 all-gather.6
  101.5 66.6 all-gather.12
  170.4 79.2 all-gather.14
  252.9 59.2 all-gather.8
  315.5 92.8 all-gather.10
  553.0 75.0 reduce-scatter.5
  630.4 84.8 reduce-scatter.9
  721.1 127.0 reduce-scatter.13
  854.3 144.8 reduce-scatter.11
  1001.5 100.7 reduce-scatter.7

commit v2 on v1

--- a/solution.py
+++ b/solution.py
@@ -120,12 +120,23 @@
             at += size
         return out
 
+    def shift_z(value, step):
+        if step % z_count == 0:
+            return value
+        pairs = [(i, (i + step) % z_count) for i in range(z_count)]
+        return lax.ppermute(value, "z", pairs)
+
+    def fetch(value):
+        return lax.all_gather(value, ("dp", "z"), axis=0, tiled=True)
+
     def gather(value):
-        own = lax.all_gather(value, ("dp", "z"), axis=0, tiled=True)
+        own = fetch(value)
         return own, swap(own)
 
-    def scatter(own, par):
+    def scatter(own, par, before=None):
         total = (own + swap(par.astype(bf16)).astype(f32)).astype(bf16)
+        if before is not None:
+            total, _ = lax.optimization_barrier((total, before))
         return lax.psum_scatter(total, ("dp", "z"), scatter_dimension=0, tiled=True)
 
     def dot(a, b):
@@ -163,9 +174,11 @@
     query_pos = lax.dynamic_slice_in_dim(pos_store, slot * token_span, token_span, 1).reshape(
         token_rows
     )
-    pairs_index = true_index.reshape(z_count, 2, token_span)
+    back = (lax.axis_index("z") - jnp.arange(z_count)) % z_count
+    pairs_index = jnp.take(true_index.reshape(z_count, 2, token_span), back, axis=0)
     key_index = order(pairs_index[:, 0], pairs_index[:, 1], axis=0).reshape(-1)
     pairs_segs = seg_store.reshape(sequence_count, z_count, 2, token_span)
+    pairs_segs = jnp.take(pairs_segs, back, axis=1)
     key_segs = order(pairs_segs[:, :, 0], pairs_segs[:, :, 1], axis=1).reshape(sequence_count, -1)
     allowed = (query_segs[:, :, None] == key_segs[:, None, :]) & (
         key_index[None, None, :] <= query_index[None, :, None]
@@ -191,7 +204,7 @@
     kv = jnp.stack([keys.reshape(values_low.shape), values_low])
     kv = kv.reshape(2, sequence_count, token_span, KEY_VALUE_HEADS, HEAD_SIZE)
     kv = kv.transpose(0, 1, 3, 2, 4)
-    kv_own = lax.all_gather(kv, "z", axis=0)
+    kv_own = jnp.stack([shift_z(kv, step) for step in range(z_count)])
     kv_all = jnp.concatenate([kv_own, swap(kv_own)], axis=0)
     kv_all = kv_all.transpose(1, 2, 3, 0, 4, 5)
     key_count = kv_all.shape[3] * token_span
@@ -199,8 +212,7 @@
     k_all, v_all = kv_all[0], kv_all[1]
 
     out_own, out_par = gather(chip_out)
-    gu_own, gu_par = gather(chip_gu)
-    down_own, down_par = gather(chip_down)
+    gu_own, down_own = fetch(chip_gu), fetch(chip_down)
 
     def to_heads(value):
         value = value.reshape(sequence_count, token_span, KEY_VALUE_HEADS, group, HEAD_SIZE)
@@ -222,6 +234,8 @@
     probs_low = probs.astype(bf16)
     mixed = jnp.einsum("shqk,shkd->shqd", probs_low, v_all, preferred_element_type=f32)
     mixed_low = from_heads(mixed.astype(bf16))
+    mixed_low, gu_own, down_own = lax.optimization_barrier((mixed_low, gu_own, down_own))
+    gu_par, down_par = swap(gu_own), swap(down_own)
 
     middle = inputs + order(dot(mixed_low, out_own), dot(mixed_low, out_par))
     normed_two = rms_scale(middle, gain_two).astype(bf16)
@@ -244,16 +258,16 @@
     dh_own, dh_par = halves(d_hidden)
     d_both_own = hidden_back_own(dh_own)[0].astype(bf16)
     d_both_par = hidden_back_par(dh_par)[0].astype(bf16)
-    s_gu = scatter(dot_tn(normed_two, d_both_own), dot_tn(normed_two, d_both_par))
+    s_gu = scatter(dot_tn(normed_two, d_both_own), dot_tn(normed_two, d_both_par), s_down)
     d_normed_two = dot_nt(d_both_own, gu_own) + dot_nt(d_both_par, gu_par)
     _, norm_two_back = jax.vjp(rms_scale, middle, gain_two)
     d_middle_norm, grad_two = norm_two_back(d_normed_two)
     d_middle = grad_out + d_middle_norm
     d_attn = d_middle.astype(bf16)
     da_own, da_par = halves(d_attn)
-    s_out = scatter(dot_tn(mixed_low, da_own), dot_tn(mixed_low, da_par))
+    s_out = scatter(dot_tn(mixed_low, da_own), dot_tn(mixed_low, da_par), s_gu)
     d_mixed = (dot_nt(da_own, out_own) + dot_nt(da_par, out_par)).astype(bf16)
-    g_heads = to_heads(d_mixed)
+    g_heads, s_down = lax.optimization_barrier((to_heads(d_mixed), s_down))
 
     d_probs = jnp.einsum("shqd,shkd->shqk", g_heads, v_all, preferred_element_type=f32)
     inner = jnp.sum(probs * d_probs, axis=-1, keepdims=True)
@@ -265,9 +279,12 @@
     terms = terms.reshape(
         2, sequence_count, KEY_VALUE_HEADS, 2 * z_count, token_span, HEAD_SIZE
     ).transpose(3, 0, 1, 2, 4, 5)
-    terms_sum = (terms[:z_count].astype(f32) + swap(terms[z_count:]).astype(f32)).astype(bf16)
-    d_kv = lax.psum_scatter(terms_sum, "z", scatter_dimension=0, tiled=False)
-    d_kv = d_kv.transpose(0, 1, 3, 2, 4).astype(f32)
+    terms_sum = terms[:z_count].astype(f32) + swap(terms[z_count:]).astype(f32)
+    d_kv = terms_sum[0]
+    for step in range(1, z_count):
+        d_kv = d_kv + shift_z(terms_sum[step].astype(bf16), -step).astype(f32)
+    d_kv, s_gu = lax.optimization_barrier((d_kv, s_gu))
+    d_kv = d_kv.transpose(0, 1, 3, 2, 4)
     d_queries = from_heads(d_queries * score_scale)
 
     _, query_back = jax.vjp(head_path, q_lin, gain_query)

time: 1120 us -> 985 us (0.88)
  waiting for transfers between devices: 821 us -> 651 us
  local copies, waits for them, and re-layouts: 61 us -> 77.7 us
  other arithmetic: 78.6 us -> 91.2 us
    all_gather x5 -> x4, waiting for transfers between devices: 349 us -> 194 us  [fetch(): return lax.all_gather(value, ('dp', 'z'), axis=0, tiled=True)]
    ppermute x0 -> x6, waiting for transfers between devices: none -> 155 us  [shift_z(): return lax.ppermute(value, 'z', pairs)]
    reduce_scatter x4, waiting for transfers between devices: 427 us -> 291 us  [scatter(): return lax.psum_scatter(total, ('dp', 'z'), scatter_dimension=0, tiled=True)]
    ppermute x18, waiting for transfers between devices: 31.1 us -> 11.3 us  [swap(): return lax.ppermute(value, 'core', SWAP)]
    reduce_scatter x1 -> x0, waiting for transfers between devices: 14 us -> none  [local(): d_kv = lax.psum_scatter(terms_sum, 'z', scatter_dimension=0, tiled=False)]
    another operation x5 -> x7, other arithmetic: 2.15 us -> 15 us
  transfers between devices with their start and end apart: 28 -> 32, of which waited for: 21 -> 19; matrix products, arithmetic and copies ran while one was open for 15% -> 28% of each run, Pallas kernels for 0% -> 0%
where the time goes in v2:
time: 985 us; the launch traced here: 976 us
  waiting for transfers between devices  651 us (66%)
  matrix products  126 us (13%)
  other arithmetic  91.2 us (9%)
  local copies, waits for them, and re-layouts  77.7 us (8%)
  between operations  16.3 us (2%)
  starting transfers between devices  13.8 us (1%)
    reduce_scatter x4, waiting for transfers between devices, scatter(): return lax.psum_scatter(total, ('dp', 'z'), scatter_dimension=0, tiled=True)  291 us
    all_gather x4, waiting for transfers between devices, fetch(): return lax.all_gather(value, ('dp', 'z'), axis=0, tiled=True)  194 us
    ppermute x6, waiting for transfers between devices, shift_z(): return lax.ppermute(value, 'z', pairs)  155 us
    dot_general x8, matrix products, dot_tn(): lax.dot_general(a, b, (((0,), (0,)), ((), ())), preferred_element_type=f32)  33.5 us
    dot_general x8, matrix products, dot_nt(): lax.dot_general(a, b, (((1,), (1,)), ((), ())), preferred_element_type=f32)  23.4 us
  transfers between devices with their start and end apart: 32, of which 19 were waited for; matrix products, arithmetic and copies ran while one was open for 28% of the time, Pallas kernels for 0%

profile of v2, /device:TPU:0, one launch (start us, length us, event | category | flops | bytes accessed | tf_op | source)
XLA Modules:
  0.0 975.5 jit_solution(4590455957062086014)
XLA Ops:
  17.6 76.0 %all-gather.5.cloned.1.call-done = bf16[1024,2176]{1,0:T(8,128)(2,1)} async-done(((bf16[64,2176]{1,0:T(8,128)(2,1)}), bf16[1024,2176]{1,0:T(8,128)(2,1)}) %all-gather.5.cloned.1.call-update) | async-done | bytes 4456464 | tf_op jit(solution)/shard_map/all_gather | solution.py:130
  96.7 2.8 gather_fusion.3
  99.7 2.8 gather_fusion.2
  108.1 3.9 fusion.82
  121.5 2.4 collective-permute-start.4
  129.9 25.6 %collective-permute-done.2 = bf16[2,2,8,128,128]{4,2,3,1,0:T(8,128)(2,1)S(1)} collective-permute-done((bf16[2,2,8,128,128]{4,2,3,1,0:T(8,128)(2,1)}, bf16[2,2,8,128,128]{4,2,3,1,0:T(8,128)(2,1)S(1)}, u32[]{:S(2)}, u32[]{:S(2)}) %collective-permute-start.2) | collective-permute-done | bytes 1048608 | tf_op jit(solution)/shard_map/ppermute | solution.py:127
  155.6 56.8 %collective-permute-done.3 = bf16[2,2,8,128,128]{4,2,3,1,0:T(8,128)(2,1)} collective-permute-done((bf16[2,2,8,128,128]{4,2,3,1,0:T(8,128)(2,1)}, bf16[2,2,8,128,128]{4,2,3,1,0:T(8,128)(2,1)}, u32[]{:S(2)}, u32[]{:S(2)}) %collective-permute-start.3) | collective-permute-done | bytes 1048608 | tf_op jit(solution)/shard_map/ppermute | solution.py:127
  212.4 3.5 pad_maximum_fusion
  220.6 1.7 slice_select_fusion.3
  225.1 1.9 multiply_multiply_fusion
  230.2 1.6 constant_dynamic-update-slice_fusion.2
  233.2 3.0 constant_dynamic-update-slice_fusion
  237.0 3.1 copy.157
  240.1 3.0 copy.156
  243.1 11.1 %fusion.80 = (f32[2,8,256]{2,1,0:T(8,128)S(1)}, f32[2,8,256,1024]{3,2,1,0:T(8,128)}) fusion(pred[2,256,1024]{2,1,0:T(8,128)(4,1)S(1)} %copy-done.63, bf16[2,8,256,128]{3,2,1,0:T(8,128)(2,1)S(1)} %bitcast.259, bf16[2,8,1024,128]{3,2,1,0:T(8,128)(2,1)} %bitcast.251), kind=kOutput, calls=%fused_computation.306 | convolution fusion | flops 1090520064 | bytes 22560768 | tf_op jit(solution)/shard_map/sub | solution.py:232
  254.2 9.8 %fusion.23 = bf16[2,8,256,128]{3,2,1,0:T(8,128)(2,1)S(1)} fusion(bf16[2,8,1024,128]{3,2,1,0:T(8,128)(2,1)} %bitcast.253, f32[2,8,256,1024]{3,2,1,0:T(8,128)} %get-tuple-element.133, f32[2,8,256]{2,1,0:T(8,128)S(1)} %get-tuple-element.132), kind=kOutput, calls=%fused_computation.70 | convolution fusion | flops 1082654720 | bytes 22036480 | tf_op jit(solution)/shard_map/shqk,shkd->shqd/dot_general | solution.py:235
  266.2 55.4 %all-gather.7.cloned.1.call-done = bf16[1024,3072]{1,0:T(8,128)(2,1)} async-done(((bf16[64,3072]{1,0:T(8,128)(2,1)}), bf16[1024,3072]{1,0:T(8,128)(2,1)}) %all-gather.7.cloned.1.call-update) | async-done | bytes 6291472 | tf_op jit(solution)/shard_map/all_gather | solution.py:130
  321.5 62.3 %all-gather.11.cloned.1.call-done = bf16[2048,512]{1,0:T(8,128)(2,1)} async-done(((bf16[128,512]{1,0:T(8,128)(2,1)}), bf16[2048,512]{1,0:T(8,128)(2,1)}) %all-gather.11.cloned.1.call-update) | async-done | bytes 2097168 | tf_op jit(solution)/shard_map/all_gather | solution.py:130
  384.3 3.9 collective-permute-done.9
  390.1 1.8 copy-done.94
  391.9 1.8 fusion.84
  393.7 4.6 fusion.85
  403.7 1.7 copy-done.37
  406.3 3.0 fusion.42
  409.4 4.5 convolution_convert_fusion
  414.0 2.8 add_convert_fusion.3
  416.9 5.7 fusion.48
  422.6 5.6 multiply_reduce_fusion.5
  431.8 1.7 fusion.12
  433.6 2.7 reshape.429
  436.3 2.6 copy.159
  438.9 7.2 add_convert_fusion
  446.1 100.0 %reduce-scatter.5.cloned.1.call-done = bf16[192,512]{1,0:T(8,128)(2,1)} async-done(((bf16[3072,512]{1,0:T(8,128)(2,1)}), bf16[192,512]{1,0:T(8,128)(2,1)}) %reduce-scatter.5.cloned.1.call-update) | async-done | bytes 196624 | tf_op jit(solution)/shard_map/reduce_scatter | solution.py:140
  547.4 7.9 fusion.9
  555.3 5.7 copy.166
  561.0 10.7 %multiply_reduce_fusion = (f32[2,8,256]{2,1,0:T(8,128)S(1)}, f32[2,8,256,1024]{3,2,1,0:T(8,128)}) fusion(f32[2,8,256,1024]{3,2,1,0:T(8,128)} %get-tuple-element.133, f32[2,8,256]{2,1,0:T(8,128)S(1)} %get-tuple-element.132, bf16[2,8,256,128]{3,2,1,0:T(8,128)(2,1)S(1)} %bitcast.273, bf16[2,8,1024,128]{3,2,1,0:T(8,128)(2,1)S(1)} %bitcast.254), kind=kOutput, calls=%fused_computation.6 | convolution fusion | flops 1086320640 | bytes 38830080 | tf_op jit(solution)/shard_map/shqd,shkd->shqk/dot_general | solution.py:272
  571.7 12.1 %multiply_convert_fusion = bf16[2,8,256,1024]{3,2,1,0:T(8,128)(2,1)S(1)} fusion(f32[2,8,256,1024]{3,2,1,0:T(8,128)} %get-tuple-element.136, f32[2,8,256]{2,1,0:T(8,128)S(1)} %get-tuple-element.135, f32[2,8,256,1024]{3,2,1,0:T(8,128)} %get-tuple-element.133, f32[2,8,256]{2,1,0:T(8,128)S(1)} %get-tuple-element.132), kind=kLoop, calls=%fused_computation.5 | loop fusion | flops 16777216 | bytes 41975808 | tf_op jit(solution)/shard_map/convert_element_type | solution.py:274
  583.8 7.0 multiply_convert_fusion.1
  590.8 7.9 copy.165
  598.7 6.4 maximum_bitcast_fusion
  605.1 2.8 slice.393
  608.6 3.6 convolution_convert_fusion.2
  612.4 4.8 convolution_multiply_fusion
  617.2 1.8 copy.160
  619.1 2.6 multiply_add_fusion.1
  621.7 8.4 fusion.73
  630.2 3.7 slice_bitcast_fusion.3
  635.3 1.7 collective-permute-start.15
  638.4 2.7 multiply_reduce_fusion.1
  645.5 4.2 fusion.13
  651.0 16.6 %collective-permute-done.16 = bf16[2,2,8,128,128]{4,2,3,1,0:T(8,128)(2,1)} collective-permute-done((bf16[2,2,8,128,128]{4,2,3,1,0:T(8,128)(2,1)}, bf16[2,2,8,128,128]{4,2,3,1,0:T(8,128)(2,1)}, u32[]{:S(2)}, u32[]{:S(2)}) %collective-permute-start.16) | collective-permute-done | bytes 1048608 | tf_op jit(solution)/shard_map/ppermute | solution.py:127
  667.6 55.8 %collective-permute-done.15 = bf16[2,2,8,128,128]{4,2,3,1,0:T(8,128)(2,1)} collective-permute-done((bf16[2,2,8,128,128]{4,2,3,1,0:T(8,128)(2,1)}, bf16[2,2,8,128,128]{4,2,3,1,0:T(8,128)(2,1)}, u32[]{:S(2)}, u32[]{:S(2)}) %collective-permute-start.15) | collective-permute-done | bytes 1048608 | tf_op jit(solution)/shard_map/ppermute | solution.py:127
  723.4 2.9 fusion.16
  726.3 22.3 %reduce-scatter.7.cloned.1.call-done = bf16[64,3072]{1,0:T(8,128)(2,1)} async-done(((bf16[1024,3072]{1,0:T(8,128)(2,1)}), bf16[64,3072]{1,0:T(8,128)(2,1)}) %reduce-scatter.7.cloned.1.call-update) | async-done | bytes 393232 | tf_op jit(solution)/shard_map/reduce_scatter | solution.py:140
  752.0 2.1 fusion.29
  755.2 3.7 fusion.43
  759.0 3.9 fusion.35
  763.2 4.9 add_convert_fusion.2
  768.0 3.6 add_convert_fusion.4
  772.1 3.8 collective-permute-done.18
  775.9 5.9 add_convert_fusion.1
  783.0 3.3 fusion.72
  791.3 72.1 %reduce-scatter.11.cloned.1.call-done = bf16[128,512]{1,0:T(8,128)(2,1)} async-done(((bf16[2048,512]{1,0:T(8,128)(2,1)}), bf16[128,512]{1,0:T(8,128)(2,1)}) %reduce-scatter.11.cloned.1.call-update) | async-done | bytes 131088 | tf_op jit(solution)/shard_map/reduce_scatter | solution.py:140
  867.1 96.6 %reduce-scatter.9.cloned.1.call-done = bf16[64,2176]{1,0:T(8,128)(2,1)} async-done(((bf16[1024,2176]{1,0:T(8,128)(2,1)}), bf16[64,2176]{1,0:T(8,128)(2,1)}) %reduce-scatter.9.cloned.1.call-update) | async-done | bytes 278544 | tf_op jit(solution)/shard_map/reduce_scatter | solution.py:140
  (411 shorter events, 91.4 us)
Async XLA Ops:
  7.2 7.9 copy-start.68
  7.2 7.9 copy-start.69
  7.2 86.4 %all-gather.5.cloned.1.call-start = ((), (), s32[]{:S(2)}) async-start(), calls=%async_computation.4 | async-start | bytes 4734976 | tf_op jit(solution)/shard_map/all_gather | solution.py:130
  9.9 1.5 collective-permute-start
  12.8 80.8 %copy-start.62 = (bf16[64,1024]{1,0:T(8,128)(2,1)S(1)}, bf16[64,1024]{1,0:T(8,128)(2,1)}, u32[]{:S(2)}) copy-start(bf16[64,1024]{1,0:T(8,128)(2,1)} %param.21) | copy-start | bytes 393220
  12.8 253.3 %all-gather.9.cloned.1.call-start = ((), (), s32[]{:S(2)}) async-start(), calls=%async_computation.6 | async-start | bytes 3342336 | tf_op jit(solution)/shard_map/all_gather | solution.py:130
  12.9 81.9 %copy-start.72 = (s32[2,1024]{1,0:T(2,128)S(1)}, s32[2,1024]{1,0:T(2,128)}, u32[]{:S(2)}) copy-start(s32[2,1024]{1,0:T(2,128)} %param.16) | copy-start | bytes 24580
  12.9 1.4 collective-permute-start.7
  15.0 81.5 %copy-start.95 = (s32[8]{0:T(128)S(1)}, s32[8]{0:T(128)}, u32[]{:S(2)}) copy-start(s32[8]{0:T(128)} %param.17) | copy-start | bytes 100
  15.0 306.5 %all-gather.7.cloned.1.call-start = ((), (), s32[]{:S(2)}) async-start(), calls=%async_computation.5 | async-start | bytes 6684672 | tf_op jit(solution)/shard_map/all_gather | solution.py:130
  15.2 1.5 collective-permute-start.6
  17.6 366.2 %all-gather.11.cloned.1.call-start = ((), (), s32[]{:S(2)}) async-start(), calls=%async_computation.7 | async-start | bytes 2228224 | tf_op jit(solution)/shard_map/all_gather | solution.py:130
  93.7 12.6 %collective-permute-start.1 = (bf16[1024,2176]{1,0:T(8,128)(2,1)}, bf16[1024,2176]{1,0:T(8,128)(2,1)}, u32[]{:S(2)}, u32[]{:S(2)}) collective-permute-start(bf16[1024,2176]{1,0:T(8,128)(2,1)} %all-gather.5.cloned.1.call-done), channel_id=1, source_target_pairs={{0,1},{1,0},{2,3},{3,2},{4,5},{5,4},{6,7},{7,6},{8,9},{9,8},{10,11... | collective-permute-start | bytes 13369352 | tf_op jit(solution)/shard_map/ppermute | solution.py:67
  94.3 124.7 %collective-permute-start.8 = (bf16[64,512]{1,0:T(8,128)(2,1)}, bf16[64,512]{1,0:T(8,128)(2,1)}, u32[]{:S(2)}, u32[]{:S(2)}) collective-permute-start(bf16[64,512]{1,0:T(8,128)(2,1)} %broadcast_select_fusion.47), channel_id=1, source_target_pairs={{0,1},{1,0},{2,3},{3,2},{4,5},{5,4},{6,7},{7,6},{8,9},{9,8},{10,11... | collective-permute-start | bytes 196616 | tf_op jit(solution)/shard_map/ppermute | solution.py:67
  94.8 8.9 copy-start.6
  96.5 27.4 %copy-start.89 = (s32[8]{0:T(128)}, s32[8]{0:T(128)S(1)}, u32[]{:S(2)}) copy-start(s32[8]{0:T(128)S(1)} %broadcast_multiply_fusion) | copy-start | bytes 100
  102.5 9.6 copy-start.40
  102.6 9.5 copy-start.79
  103.9 8.2 copy-start.80
  103.9 8.2 copy-start.82
  105.1 121.9 %copy-start.33 = (f32[256,64]{1,0:T(8,128)}, f32[256,64]{1,0:T(8,128)S(1)}, u32[]{:S(2)}) copy-start(f32[256,64]{1,0:T(8,128)S(1)} %get-tuple-element.130) | copy-start | bytes 196612
  105.1 121.9 %copy-start.35 = (f32[256,64]{1,0:T(8,128)}, f32[256,64]{1,0:T(8,128)S(1)}, u32[]{:S(2)}) copy-start(f32[256,64]{1,0:T(8,128)S(1)} %get-tuple-element.131) | copy-start | bytes 196612
  117.4 6.5 copy-start.78
  119.0 36.6 %collective-permute-start.2 = (bf16[2,2,8,128,128]{4,2,3,1,0:T(8,128)(2,1)}, bf16[2,2,8,128,128]{4,2,3,1,0:T(8,128)(2,1)S(1)}, u32[]{:S(2)}, u32[]{:S(2)}) collective-permute-start(bf16[2,2,8,128,128]{4,2,3,1,0:T(8,128)(2,1)} %get-tuple-element.76), channel_id=1, source_target_pairs={{0,2},{2,4},{4,6},{6,0},{1,3},{3,5},{5,7},{7,1},{8,10},{10,12},{12... | collective-permute-start | bytes 3145736 | tf_op jit(solution)/shard_map/ppermute | solution.py:127
  120.5 91.8 %collective-permute-start.3 = (bf16[2,2,8,128,128]{4,2,3,1,0:T(8,128)(2,1)}, bf16[2,2,8,128,128]{4,2,3,1,0:T(8,128)(2,1)}, u32[]{:S(2)}, u32[]{:S(2)}) collective-permute-start(bf16[2,2,8,128,128]{4,2,3,1,0:T(8,128)(2,1)} %get-tuple-element.76), channel_id=1, source_target_pairs={{0,4},{2,6},{4,0},{6,2},{1,5},{3,7},{5,1},{7,3},{8,12},{10,14},{12... | collective-permute-start | bytes 3145736 | tf_op jit(solution)/shard_map/ppermute | solution.py:127
  121.5 90.8 %collective-permute-start.4 = (bf16[2,2,8,128,128]{4,2,3,1,0:T(8,128)(2,1)}, bf16[2,2,8,128,128]{4,2,3,1,0:T(8,128)(2,1)}, u32[]{:S(2)}, u32[]{:S(2)}) collective-permute-start(bf16[2,2,8,128,128]{4,2,3,1,0:T(8,128)(2,1)} %get-tuple-element.76), channel_id=1, source_target_pairs={{0,6},{2,0},{4,2},{6,4},{1,7},{3,1},{5,3},{7,5},{8,14},{10,8},{12,... | collective-permute-start | bytes 3145736 | tf_op jit(solution)/shard_map/ppermute | solution.py:127
  155.6 60.3 %copy-start.31 = (bf16[2,2,8,128,128]{4,2,3,1,0:T(8,128)(2,1)}, bf16[2,2,8,128,128]{4,2,3,1,0:T(8,128)(2,1)S(1)}, u32[]{:S(2)}) copy-start(bf16[2,2,8,128,128]{4,2,3,1,0:T(8,128)(2,1)S(1)} %collective-permute-done.2) | copy-start | bytes 3145732
  215.8 17.3 %collective-permute-start.5 = (bf16[4,2,2,8,128,128]{5,3,4,2,1,0:T(8,128)(2,1)}, bf16[4,2,2,8,128,128]{5,3,4,2,1,0:T(8,128)(2,1)}, u32[]{:S(2)}, u32[]{:S(2)}) collective-permute-start(bf16[4,2,2,8,128,128]{5,3,4,2,1,0:T(8,128)(2,1)} %pad_maximum_fusion), channel_id=1, source_target_pairs={{0,1},{1,0},{2,3},{3,2},{4,5},{5,4},{6,7},{7,6},{8,9},{9,8},{10,11... | collective-permute-start | bytes 12582920 | tf_op jit(solution)/shard_map/ppermute | solution.py:67
  220.5 325.6 %reduce-scatter.5.cloned.1.call-start = ((), (), s32[]{:S(2)}) async-start(), calls=%async_computation.8 | async-start | bytes 3342336 | tf_op jit(solution)/shard_map/reduce_scatter | solution.py:140
  230.1 13.0 %copy-start.30 = (bf16[2,128,8,2,128]{4,1,3,2,0:T(8,128)(2,1)}, bf16[2,128,8,2,128]{4,1,3,2,0:T(8,128)(2,1)S(1)}, u32[]{:S(2)}) copy-start(bf16[2,128,8,2,128]{4,1,3,2,0:T(8,128)(2,1)S(1)} %pad_maximum_fusion.2) | copy-start | bytes 3145732
  266.1 123.5 %copy-start.9 = (bf16[256,2048]{1,0:T(8,128)(2,1)}, bf16[256,2048]{1,0:T(8,128)(2,1)S(1)}, u32[]{:S(2)}) copy-start(bf16[256,2048]{1,0:T(8,128)(2,1)S(1)} %reshape.427) | copy-start | bytes 3145732
  321.5 72.2 %collective-permute-start.10 = (bf16[1024,3072]{1,0:T(8,128)(2,1)}, bf16[1024,3072]{1,0:T(8,128)(2,1)}, u32[]{:S(2)}, u32[]{:S(2)}) collective-permute-start(bf16[1024,3072]{1,0:T(8,128)(2,1)} %all-gather.7.cloned.1.call-done), channel_id=1, source_target_pairs={{0,1},{1,0},{2,3},{3,2},{4,5},{5,4},{6,7},{7,6},{8,9},{9,8},{10,11... | collective-permute-start | bytes 18874376 | tf_op jit(solution)/shard_map/ppermute | solution.py:67
  383.8 4.4 collective-permute-start.9
  383.8 19.8 %collective-permute-start.11 = (bf16[3072,512]{1,0:T(8,128)(2,1)}, bf16[3072,512]{1,0:T(8,128)(2,1)S(1)}, u32[]{:S(2)}, u32[]{:S(2)}) collective-permute-start(bf16[3072,512]{1,0:T(8,128)(2,1)} %all-gather.9.cloned.1.call-done), channel_id=1, source_target_pairs={{0,1},{1,0},{2,3},{3,2},{4,5},{5,4},{6,7},{7,6},{8,9},{9,8},{10,11... | collective-permute-start | bytes 9437192 | tf_op jit(solution)/shard_map/ppermute | solution.py:67
  389.6 38.6 %copy-start.13 = (f32[256,512]{1,0:T(8,128)}, f32[256,512]{1,0:T(8,128)S(1)}, u32[]{:S(2)}) copy-start(f32[256,512]{1,0:T(8,128)S(1)} %get-tuple-element.74) | copy-start | bytes 1572868
  399.3 14.7 %copy-start.52 = (bf16[256,1536]{1,0:T(8,128)(2,1)}, bf16[256,1536]{1,0:T(8,128)(2,1)S(1)}, u32[]{:S(2)}) copy-start(bf16[256,1536]{1,0:T(8,128)(2,1)S(1)} %get-tuple-element.39) | copy-start | bytes 2359300
  399.4 14.6 %copy-start.54 = (bf16[256,1536]{1,0:T(8,128)(2,1)}, bf16[256,1536]{1,0:T(8,128)(2,1)S(1)}, u32[]{:S(2)}) copy-start(bf16[256,1536]{1,0:T(8,128)(2,1)S(1)} %broadcast_select_fusion) | copy-start | bytes 2359300
  401.7 12.3 %collective-permute-start.12 = (bf16[3072,512]{1,0:T(8,128)(2,1)S(1)}, bf16[3072,512]{1,0:T(8,128)(2,1)S(1)}, u32[]{:S(2)}, u32[]{:S(2)}) collective-permute-start(bf16[3072,512]{1,0:T(8,128)(2,1)S(1)} %convolution_convert_fusion.1), channel_id=1, source_target_pairs={{0,1},{1,0},{2,3},{3,2},{4,5},{5,4},{6,7},{7,6},{8,9},{9,8},{10,11... | collective-permute-start | bytes 9437192 | tf_op jit(solution)/shard_map/ppermute | solution.py:67
  413.9 25.0 %collective-permute-start.17 = (bf16[1024,3072]{1,0:T(8,128)(2,1)}, bf16[1024,3072]{1,0:T(8,128)(2,1)}, u32[]{:S(2)}, u32[]{:S(2)}) collective-permute-start(bf16[1024,3072]{1,0:T(8,128)(2,1)} %convolution_convert_fusion), channel_id=1, source_target_pairs={{0,1},{1,0},{2,3},{3,2},{4,5},{5,4},{6,7},{7,6},{8,9},{9,8},{10,11... | collective-permute-start | bytes 18874376 | tf_op jit(solution)/shard_map/ppermute | solution.py:67
  416.8 331.7 %reduce-scatter.7.cloned.1.call-start = ((), (), s32[]{:S(2)}) async-start(), calls=%async_computation.9 | async-start | bytes 6684672 | tf_op jit(solution)/shard_map/reduce_scatter | solution.py:140
  546.2 317.1 %reduce-scatter.11.cloned.1.call-start = ((), (), s32[]{:S(2)}) async-start(), calls=%async_computation.11 | async-start | bytes 2228224 | tf_op jit(solution)/shard_map/reduce_scatter | solution.py:140
  555.3 5.7 copy-start.28
  583.8 7.0 copy-start.4
  590.8 7.9 copy-start.12
  598.7 9.9 %copy-start.10 = (bf16[256,2048]{1,0:T(8,128)(2,1)S(1)}, bf16[256,2048]{1,0:T(8,128)(2,1)}, u32[]{:S(2)}) copy-start(bf16[256,2048]{1,0:T(8,128)(2,1)} %copy-done.9) | copy-start | bytes 3145732
  605.1 7.3 copy-start.5
  607.9 13.8 %collective-permute-start.13 = (bf16[4,2,2,8,128,128]{5,3,4,2,1,0:T(8,128)(2,1)S(1)}, bf16[4,2,2,8,128,128]{5,3,4,2,1,0:T(8,128)(2,1)}, u32[]{:S(2)}, u32[]{:S(2)}) collective-permute-start(bf16[4,2,2,8,128,128]{5,3,4,2,1,0:T(8,128)(2,1)S(1)} %slice.393), channel_id=1, source_target_pairs={{0,1},{1,0},{2,3},{3,2},{4,5},{5,4},{6,7},{7,6},{8,9},{9,8},{10,11... | collective-permute-start | bytes 12582920 | tf_op jit(solution)/shard_map/ppermute | solution.py:67
  608.6 13.1 %slice-start = ((s8[8388608]{0:T(1024)(128)(4,1)}), s8[4194304]{0:T(1024)(128)(4,1)S(1)}, s32[]{:S(2)}) async-start(s8[8388608]{0:T(1024)(128)(4,1)} %bitcast.232), calls=%async_computation.12 | async-start | bytes 8388608
  612.2 9.5 slice-start.1
  612.2 155.9 %collective-permute-start.20 = (bf16[2048,512]{1,0:T(8,128)(2,1)}, bf16[2048,512]{1,0:T(8,128)(2,1)}, u32[]{:S(2)}, u32[]{:S(2)}) collective-permute-start(bf16[2048,512]{1,0:T(8,128)(2,1)} %convolution_convert_fusion.2), channel_id=1, source_target_pairs={{0,1},{1,0},{2,3},{3,2},{4,5},{5,4},{6,7},{7,6},{8,9},{9,8},{10,11... | collective-permute-start | bytes 6291464 | tf_op jit(solution)/shard_map/ppermute | solution.py:67
  621.7 16.7 %copy-start.42 = (f32[256,16]{1,0:T(8,128)S(1)}, f32[256,16]{1,0:T(8,128)}, u32[]{:S(2)}) copy-start(f32[256,16]{1,0:T(8,128)} %copy-done.41) | copy-start | bytes 49156
  630.2 8.3 copy-start.1
  630.2 8.3 copy-start.7
  630.2 8.3 copy-start.8
  630.2 8.3 copy-start.86
  633.9 33.8 %collective-permute-start.16 = (bf16[2,2,8,128,128]{4,2,3,1,0:T(8,128)(2,1)}, bf16[2,2,8,128,128]{4,2,3,1,0:T(8,128)(2,1)}, u32[]{:S(2)}, u32[]{:S(2)}) collective-permute-start(bf16[2,2,8,128,128]{4,2,3,1,0:T(8,128)(2,1)} %get-tuple-element.57), channel_id=1, source_target_pairs={{0,2},{2,4},{4,6},{6,0},{1,3},{3,5},{5,7},{7,1},{8,10},{10,12},{12... | collective-permute-start | bytes 3145736 | tf_op jit(solution)/shard_map/ppermute | solution.py:127
  635.3 88.1 %collective-permute-start.15 = (bf16[2,2,8,128,128]{4,2,3,1,0:T(8,128)(2,1)}, bf16[2,2,8,128,128]{4,2,3,1,0:T(8,128)(2,1)}, u32[]{:S(2)}, u32[]{:S(2)}) collective-permute-start(bf16[2,2,8,128,128]{4,2,3,1,0:T(8,128)(2,1)} %get-tuple-element.58), channel_id=1, source_target_pairs={{0,4},{2,6},{4,0},{6,2},{1,5},{3,7},{5,1},{7,3},{8,12},{10,14},{12... | collective-permute-start | bytes 3145736 | tf_op jit(solution)/shard_map/ppermute | solution.py:127
  636.9 86.4 %collective-permute-start.14 = (bf16[2,2,8,128,128]{4,2,3,1,0:T(8,128)(2,1)}, bf16[2,2,8,128,128]{4,2,3,1,0:T(8,128)(2,1)}, u32[]{:S(2)}, u32[]{:S(2)}) collective-permute-start(bf16[2,2,8,128,128]{4,2,3,1,0:T(8,128)(2,1)} %get-tuple-element.56), channel_id=1, source_target_pairs={{0,6},{2,0},{4,2},{6,4},{1,7},{3,1},{5,3},{7,5},{8,14},{10,8},{12,... | collective-permute-start | bytes 3145736 | tf_op jit(solution)/shard_map/ppermute | solution.py:127
  768.0 7.9 collective-permute-start.18
  771.7 192.1 %reduce-scatter.9.cloned.1.call-start = ((), (), s32[]{:S(2)}) async-start(), calls=%async_computation.10 | async-start | bytes 4734976 | tf_op jit(solution)/shard_map/reduce_scatter | solution.py:140
  787.4 1.4 collective-permute-start.23
  789.6 1.7 collective-permute-start.22
  864.2 1.3 collective-permute-start.21
  964.8 1.4 collective-permute-start.19
  (66 other events, 181.3 us)
Sparse Core Ops, SparseCore 0:
  12.9 80.6 all-gather.4
  97.1 123.0 all-gather.8
  223.6 97.8 all-gather.6
  324.8 59.0 all-gather.10
  417.0 129.1 reduce-scatter.4
  551.2 197.2 reduce-scatter.6
  771.8 91.4 reduce-scatter.10
  865.6 98.0 reduce-scatter.8
